TPU v7x, 128 devices: a whole 4x4x4 slice. The times are simulated.
128 devices in a mesh: dp: 16 (over x, y_lo, core), tensor: 8 (over z, y_hi).
Axes of the slice: x: 4, y: 4 (y_hi: 2, y_lo: 2; y = y_hi * 2 + y_lo), z: 4, core: 2. Of those that a mesh axis runs over, the one named last changes fastest.
Arguments:
- tokens: bfloat16 [8192, 2048], P('dp'), may hold values from -6 to 6
- cotangent: bfloat16 [8192, 2048], P('dp'), may hold values from -6 to 6
- group_sizes: int32 [16], P('dp'), may hold values from 4 to 16
- prefix_lens: int32 [16], P('dp'), may hold values from 64 to 128, as said below
- solution_lens: int32 [16, 16], P('dp'), may hold values from 1 to 445, as said below
- w_qkv: float32 [3, 2048, 2048], P(None, 'dp', 'tensor'), may hold values from -0.125 to 0.125
- w_out: float32 [2048, 2048], P('tensor', 'dp'), may hold values from -1 to 1
- w_up: float32 [2048, 8192], P('dp', 'tensor'), may hold values from -0.125 to 0.125
- w_down: float32 [8192, 2048], P('tensor', 'dp'), may hold values from -0.25 to 0.25
- norms: float32 [4, 2048], P(None, 'dp'), may hold values from -0.9 to 1.5, as said below
- first_qkv: float32 [3, 2048, 2048], P(None, 'dp', 'tensor'), as said below
- second_qkv: float32 [3, 2048, 2048], P(None, 'dp', 'tensor'), as said below
- first_out: float32 [2048, 2048], P('tensor', 'dp'), as said below
- second_out: float32 [2048, 2048], P('tensor', 'dp'), as said below
- first_up: float32 [2048, 8192], P('dp', 'tensor'), as said below
- second_up: float32 [2048, 8192], P('dp', 'tensor'), as said below
- first_down: float32 [8192, 2048], P('tensor', 'dp'), as said below
- second_down: float32 [8192, 2048], P('tensor', 'dp'), as said below
- first_norms: float32 [4, 2048], P(None, 'dp'), as said below
- second_norms: float32 [4, 2048], P(None, 'dp'), as said below
Outputs:
- block_out: bfloat16 [8192, 2048], P('dp')
- input_grad: float32 [8192, 2048], P('dp')
- grad_w_qkv: float32 [3, 2048, 2048], P(None, 'dp', 'tensor')
- new_first_qkv: float32 [3, 2048, 2048], P(None, 'dp', 'tensor')
- new_second_qkv: float32 [3, 2048, 2048], P(None, 'dp', 'tensor')
- new_w_qkv: float32 [3, 2048, 2048], P(None, 'dp', 'tensor')
- copy_w_qkv: bfloat16 [3, 2048, 2048], P(None, 'dp', 'tensor')
- grad_w_out: float32 [2048, 2048], P('tensor', 'dp')
- new_first_out: float32 [2048, 2048], P('tensor', 'dp')
- new_second_out: float32 [2048, 2048], P('tensor', 'dp')
- new_w_out: float32 [2048, 2048], P('tensor', 'dp')
- copy_w_out: bfloat16 [2048, 2048], P('tensor', 'dp')
- grad_w_up: float32 [2048, 8192], P('dp', 'tensor')
- new_first_up: float32 [2048, 8192], P('dp', 'tensor')
- new_second_up: float32 [2048, 8192], P('dp', 'tensor')
- new_w_up: float32 [2048, 8192], P('dp', 'tensor')
- copy_w_up: bfloat16 [2048, 8192], P('dp', 'tensor')
- grad_w_down: float32 [8192, 2048], P('tensor', 'dp')
- new_first_down: float32 [8192, 2048], P('tensor', 'dp')
- new_second_down: float32 [8192, 2048], P('tensor', 'dp')
- new_w_down: float32 [8192, 2048], P('tensor', 'dp')
- copy_w_down: bfloat16 [8192, 2048], P('tensor', 'dp')
- grad_norms: float32 [4, 2048], P(None, 'dp')
- new_first_norms: float32 [4, 2048], P(None, 'dp')
- new_second_norms: float32 [4, 2048], P(None, 'dp')
- new_norms: float32 [4, 2048], P(None, 'dp')
- copy_norms: bfloat16 [4, 2048], P(None, 'dp')
Inputs may be any that keep to these rules, and one draw needn't show every extreme that they name: `prefix_lens`: the shared prefix of a group. `solution_lens`: only the first group_sizes[g] slots of row g count. The prefix and those solutions fill between 256 and 512 positions of their group, exactly 512 in some group; the remaining positions are padding. `norms`: gains lie between 0.5 and 1.5, shifts between -0.9 and 0.9. `first_qkv`: no entry is zero. `second_qkv`: all entries are positive. `first_out`: no entry is zero. `second_out`: all entries are positive. `first_up`: no entry is zero. `second_up`: all entries are positive. `first_down`: no entry is zero. `second_down`: all entries are positive. `first_norms`: no entry is zero. `second_norms`: all entries are positive.
All inputs are finite; a program needn't handle non-finite values.
Results may differ from a plain program's by a relative error of at most 0.014.
The roundings to bfloat16 on the way count: a program that leaves them out, or rounds other values in their place, can miss the bound.
Values may be sent and summed in bfloat16 or wider, within the bound.
A program may use at most 128 MiB of HBM per device.

v0:
```python
import jax
import jax.numpy as jnp
from jax import lax
from jax.sharding import PartitionSpec as P

HD = 128
STEP = 5


NEG_FILL = -1e30
BETA_ONE = 0.5
BETA_TWO = 0.5
ADAM_EPS = 1e-08
NORM_EPS = 1e-05
DECAY_RATE = 0.1
RATE_QKV = 0.02
RATE_OUT = 0.15
RATE_UP = 0.02
RATE_DOWN = 0.01
RATE_NORMS = 0.3


def layer_norm(inputs, norm_gain, norm_shift):
    row_mean = jnp.mean(inputs, axis=-1, keepdims=True)
    centered = inputs - row_mean
    spread = jnp.mean(centered * centered, axis=-1, keepdims=True)
    return centered * lax.rsqrt(spread + NORM_EPS) * norm_gain + norm_shift


def layout(group_size, prefix_len, slot_lens, length):
    slot_count = slot_lens.shape[0]
    slot_live = jnp.arange(slot_count, dtype=jnp.int32) < group_size
    counted = jnp.where(slot_live, slot_lens, 0)
    seg_ends = prefix_len + jnp.cumsum(counted)
    position = jnp.arange(length, dtype=jnp.int32)
    segment = jnp.sum((position[:, None] >= seg_ends[None, :]).astype(jnp.int32), axis=1)
    segment = jnp.where(position < prefix_len, -1, segment)
    valid_rows = position < seg_ends[slot_count - 1]
    linked = (segment[:, None] == segment[None, :]) | (segment[None, :] < 0)
    causal = position[None, :] <= position[:, None]
    allowed = linked & causal & valid_rows[:, None] & valid_rows[None, :]
    allowed = allowed | (position[:, None] == position[None, :])
    return (allowed, valid_rows)


def adamw(weight, grad_in, first_old, second_old, step_rate, weight_decay):
    first_new = BETA_ONE * first_old + (1.0 - BETA_ONE) * grad_in
    second_new = BETA_TWO * second_old + (1.0 - BETA_TWO) * grad_in * grad_in
    corr_one = 1.0 - BETA_ONE**STEP
    corr_two = 1.0 - BETA_TWO**STEP
    step_dir = first_new / corr_one / (jnp.sqrt(second_new / corr_two) + ADAM_EPS)
    weight_new = weight - step_rate * (step_dir + weight_decay * weight)
    return (grad_in, first_new, second_new, weight_new, weight_new.astype(jnp.bfloat16))


def masked_scores(head_q, head_k, allowed):
    scores = jnp.einsum("qhd,khd->hqk", head_q, head_k, preferred_element_type=jnp.float32)
    return jnp.where(allowed[None, :, :], scores, NEG_FILL)


def per_device(
    tokens,
    cotangent,
    group_sizes,
    prefix_lens,
    solution_lens,
    w_qkv,
    w_out,
    w_up,
    w_down,
    norms,
    first_qkv,
    second_qkv,
    first_out,
    second_out,
    first_up,
    second_up,
    first_down,
    second_down,
    first_norms,
    second_norms,
):
    length = tokens.shape[0]
    allowed, valid_rows = layout(group_sizes[0], prefix_lens[0], solution_lens[0], length)
    qkv_all, out_all, up_all, down_all, norms_all = (
        lax.all_gather(w_qkv.astype(jnp.bfloat16), "dp", axis=1, tiled=True),
        lax.all_gather(w_out.astype(jnp.bfloat16), "dp", axis=1, tiled=True),
        lax.all_gather(w_up.astype(jnp.bfloat16), "dp", axis=0, tiled=True),
        lax.all_gather(w_down.astype(jnp.bfloat16), "dp", axis=1, tiled=True),
        lax.all_gather(norms.astype(jnp.bfloat16), "dp", axis=1, tiled=True),
    )
    gain_rows = norms_all.astype(jnp.float32)
    local_width = qkv_all.shape[2]
    local_heads = local_width // HD
    score_scale = HD ** (-0.5)
    inputs = tokens.astype(jnp.float32)
    normed_one = layer_norm(inputs, gain_rows[0], gain_rows[1]).astype(jnp.bfloat16)
    projected = jnp.einsum("sd,cde->cse", normed_one, qkv_all, preferred_element_type=jnp.float32)
    queries = (projected[0] * score_scale).astype(jnp.bfloat16)
    key_rows = projected[1].astype(jnp.bfloat16)
    value_rows = projected[2].astype(jnp.bfloat16)
    head_q = queries.reshape(length, local_heads, HD)
    head_k = key_rows.reshape(length, local_heads, HD)
    head_v = value_rows.reshape(length, local_heads, HD)
    scores = masked_scores(head_q, head_k, allowed)
    row_top = jnp.max(scores, axis=-1, keepdims=True)
    weights = jnp.exp(scores - row_top)
    row_total = jnp.sum(weights, axis=-1, keepdims=True)
    log_total = row_top + jnp.log(row_total)
    probs_low = (weights / row_total).astype(jnp.bfloat16)
    mixed = jnp.einsum("hqk,khd->qhd", probs_low, head_v, preferred_element_type=jnp.float32)
    mixed_low = mixed.reshape(length, local_width).astype(jnp.bfloat16)
    attn_terms = jnp.dot(mixed_low, out_all, preferred_element_type=jnp.float32)
    resid_one = inputs + lax.psum(attn_terms, "tensor")
    normed_two = layer_norm(resid_one, gain_rows[2], gain_rows[3]).astype(jnp.bfloat16)
    up_pre = jnp.dot(normed_two, up_all, preferred_element_type=jnp.float32)
    gelu_value, gelu_back = jax.vjp(lambda field: jax.nn.gelu(field, approximate=True), up_pre)
    hidden = gelu_value.astype(jnp.bfloat16)
    down_terms = jnp.dot(hidden, down_all, preferred_element_type=jnp.float32)
    back_rows = (cotangent.astype(jnp.float32) * valid_rows[:, None].astype(jnp.float32)).astype(
        jnp.bfloat16
    )
    d_hidden = jnp.einsum("sd,fd->sf", back_rows, down_all, preferred_element_type=jnp.float32)
    d_up = gelu_back(d_hidden)[0].astype(jnp.bfloat16)
    entry_terms = jnp.einsum("sf,df->sd", d_up, up_all, preferred_element_type=jnp.float32)
    block_out = (resid_one + lax.psum(down_terms, "tensor")).astype(jnp.bfloat16)
    d_normed_two = lax.psum(entry_terms, "tensor")
    norm_two_back = jax.vjp(layer_norm, resid_one, gain_rows[2], gain_rows[3])[1]
    d_resid_norm, d_gain_two, d_shift_two = norm_two_back(d_normed_two)
    d_resid = back_rows.astype(jnp.float32) + d_resid_norm
    d_attn = d_resid.astype(jnp.bfloat16)
    d_mixed = jnp.einsum("sd,ed->se", d_attn, out_all, preferred_element_type=jnp.float32).astype(
        jnp.bfloat16
    )
    d_head = d_mixed.reshape(length, local_heads, HD)
    probs = jnp.exp(masked_scores(head_q, head_k, allowed) - log_total)
    probs_again = probs.astype(jnp.bfloat16)
    d_values = jnp.einsum("hqk,qhd->khd", probs_again, d_head, preferred_element_type=jnp.float32)
    d_probs = jnp.einsum("qhd,khd->hqk", d_head, head_v, preferred_element_type=jnp.float32)
    row_delta = jnp.sum(probs * d_probs, axis=-1, keepdims=True)
    d_scores = (probs * (d_probs - row_delta)).astype(jnp.bfloat16)
    d_queries = jnp.einsum("hqk,khd->qhd", d_scores, head_k, preferred_element_type=jnp.float32)
    d_keys = jnp.einsum("hqk,qhd->khd", d_scores, head_q, preferred_element_type=jnp.float32)
    d_qkv = jnp.stack(
        [
            d_queries.reshape(length, local_width),
            d_keys.reshape(length, local_width),
            d_values.reshape(length, local_width),
        ],
        axis=1,
    ).astype(jnp.bfloat16)
    qkv_scales = jnp.array([score_scale, 1.0, 1.0], jnp.float32)
    d_parts = jnp.einsum("sce,cde->csd", d_qkv, qkv_all, preferred_element_type=jnp.float32)
    d_normed_one = lax.psum(d_parts[0] * score_scale + d_parts[1] + d_parts[2], "tensor")
    norm_one_back = jax.vjp(layer_norm, inputs, gain_rows[0], gain_rows[1])[1]
    d_input_norm, d_gain_one, d_shift_one = norm_one_back(d_normed_one)
    input_grad = d_resid + d_input_norm
    d_norm_rows = jnp.stack([d_gain_one, d_shift_one, d_gain_two, d_shift_two], axis=0)
    local_qkv = jnp.einsum("sd,sce->cde", normed_one, d_qkv, preferred_element_type=jnp.float32)
    local_qkv = local_qkv * qkv_scales[:, None, None]
    local_out = jnp.einsum("se,sd->ed", mixed_low, d_attn, preferred_element_type=jnp.float32)
    local_up = jnp.einsum("sd,sf->df", normed_two, d_up, preferred_element_type=jnp.float32)
    local_down = jnp.einsum("sf,sd->fd", hidden, back_rows, preferred_element_type=jnp.float32)
    grad_qkv, grad_out, grad_up, grad_down, grad_norm_rows = (
        lax.psum_scatter(local_qkv, "dp", scatter_dimension=1, tiled=True),
        lax.psum_scatter(local_out, "dp", scatter_dimension=1, tiled=True),
        lax.psum_scatter(local_up, "dp", scatter_dimension=0, tiled=True),
        lax.psum_scatter(local_down, "dp", scatter_dimension=1, tiled=True),
        lax.psum_scatter(d_norm_rows, "dp", scatter_dimension=1, tiled=True),
    )
    qkv_res = adamw(w_qkv, grad_qkv, first_qkv, second_qkv, RATE_QKV, DECAY_RATE)
    out_res = adamw(w_out, grad_out, first_out, second_out, RATE_OUT, DECAY_RATE)
    up_res = adamw(w_up, grad_up, first_up, second_up, RATE_UP, DECAY_RATE)
    down_res = adamw(w_down, grad_down, first_down, second_down, RATE_DOWN, DECAY_RATE)
    norm_res = adamw(norms, grad_norm_rows, first_norms, second_norms, RATE_NORMS, 0.0)
    return (
        block_out,
        input_grad,
        qkv_res[0],
        qkv_res[1],
        qkv_res[2],
        qkv_res[3],
        qkv_res[4],
        out_res[0],
        out_res[1],
        out_res[2],
        out_res[3],
        out_res[4],
        up_res[0],
        up_res[1],
        up_res[2],
        up_res[3],
        up_res[4],
        down_res[0],
        down_res[1],
        down_res[2],
        down_res[3],
        down_res[4],
        norm_res[0],
        norm_res[1],
        norm_res[2],
        norm_res[3],
        norm_res[4],
    )


def solution(mesh):
    return jax.shard_map(
        per_device,
        mesh=mesh,
        in_specs=(
            P("dp", None),
            P("dp", None),
            P("dp"),
            P("dp"),
            P("dp", None),
            P(None, "dp", "tensor"),
            P("tensor", "dp"),
            P("dp", "tensor"),
            P("tensor", "dp"),
            P(None, "dp"),
            P(None, "dp", "tensor"),
            P(None, "dp", "tensor"),
            P("tensor", "dp"),
            P("tensor", "dp"),
            P("dp", "tensor"),
            P("dp", "tensor"),
            P("tensor", "dp"),
            P("tensor", "dp"),
            P(None, "dp"),
            P(None, "dp"),
        ),
        out_specs=(
            P("dp", None),
            P("dp", None),
            P(None, "dp", "tensor"),
            P(None, "dp", "tensor"),
            P(None, "dp", "tensor"),
            P(None, "dp", "tensor"),
            P(None, "dp", "tensor"),
            P("tensor", "dp"),
            P("tensor", "dp"),
            P("tensor", "dp"),
            P("tensor", "dp"),
            P("tensor", "dp"),
            P("dp", "tensor"),
            P("dp", "tensor"),
            P("dp", "tensor"),
            P("dp", "tensor"),
            P("dp", "tensor"),
            P("tensor", "dp"),
            P("tensor", "dp"),
            P("tensor", "dp"),
            P("tensor", "dp"),
            P("tensor", "dp"),
            P(None, "dp"),
            P(None, "dp"),
            P(None, "dp"),
            P(None, "dp"),
            P(None, "dp"),
        ),
        check_vma=False,
    )
```

profile of v0, /device:TPU:1, one launch (start us, length us, event | category | flops | bytes accessed | tf_op | source)
XLA Modules:
  0.0 1361.8 jit_solution(16278582881127906931)
XLA Ops:
  11.7 21.0 %all_gather.15 = bf16[4,2048]{1,0:T(4,128)(2,1)S(1)} all-gather(bf16[4,128]{1,0:T(4,128)(2,1)S(1)} %convert_element_type.114), channel_id=1, replica_groups=mesh['dp'=16,'tensor'=8] {'dp'}, dimensions={1}, use_global_device_ids=true | all-gather | bytes 17408 | tf_op jit(solution)/shard_map/all_gather | solution.py:90
  39.1 15.9 %all-gather.5.cloned.1.call-done = bf16[3,2048,256]{1,2,0:T(8,128)(2,1)} async-done(((bf16[3,128,256]{1,2,0:T(8,128)(2,1)}), bf16[3,2048,256]{1,2,0:T(8,128)(2,1)}) %all-gather.5.cloned.1.call-update) | async-done | bytes 3145744 | tf_op jit(solution)/shard_map/all_gather | solution.py:86
  55.0 3.9 fusion.70
  61.6 29.9 %all-gather.7.cloned.1.call-done = bf16[256,2048]{1,0:T(8,128)(2,1)} async-done(((bf16[256,128]{1,0:T(8,128)(2,1)}), bf16[256,2048]{1,0:T(8,128)(2,1)}) %all-gather.7.cloned.1.call-update) | async-done | bytes 1048592 | tf_op jit(solution)/shard_map/all_gather | solution.py:87
  91.6 4.0 fusion.71
  98.7 181.7 %all-reduce.5.cloned.1.call-done = f32[512,2048]{1,0:T(8,128)} async-done(((f32[512,2048]{1,0:T(8,128)}), f32[512,2048]{1,0:T(8,128)}) %all-reduce.5.cloned.1.call-update) | async-done | bytes 4194320 | tf_op jit(solution)/shard_map/psum | solution.py:114
  286.8 32.6 %all-gather.9.cloned.1.call-done = bf16[2048,1024]{1,0:T(8,128)(2,1)} async-done(((bf16[128,1024]{1,0:T(8,128)(2,1)}), bf16[2048,1024]{1,0:T(8,128)(2,1)}) %all-gather.9.cloned.1.call-update) | async-done | bytes 4194320 | tf_op jit(solution)/shard_map/all_gather | solution.py:88
  319.4 6.0 fusion.53
  326.7 6.0 fusion.48
  333.2 95.8 %reduce-scatter.14.cloned.1.call-done = f32[1024,128]{1,0:T(8,128)} async-done(((f32[1024,2048]{1,0:T(8,128)}), f32[1024,128]{1,0:T(8,128)}) %reduce-scatter.14.cloned.1.call-update) | async-done | bytes 524304 | tf_op jit(solution)/shard_map/reduce_scatter | solution.py:168
  432.4 46.6 %all-gather.11.cloned.1.call-done = bf16[1024,2048]{1,0:T(8,128)(2,1)} async-done(((bf16[1024,128]{1,0:T(8,128)(2,1)}), bf16[1024,2048]{1,0:T(8,128)(2,1)}) %all-gather.11.cloned.1.call-update) | async-done | bytes 4194320 | tf_op jit(solution)/shard_map/all_gather | solution.py:89
  479.0 7.0 fusion.19
  487.0 4.3 fusion.72
  492.7 7.3 fusion.49
  500.0 176.2 %all-reduce.7.cloned.1.call-done = f32[512,2048]{1,0:T(8,128)} async-done(((f32[512,2048]{1,0:T(8,128)}), f32[512,2048]{1,0:T(8,128)}) %all-reduce.7.cloned.1.call-update) | async-done | bytes 4194320 | tf_op jit(solution)/shard_map/psum | solution.py:127
  676.2 5.4 multiply_reduce_fusion
  707.5 337.6 %all-reduce.9.cloned.1.call-done = (f32[512,2048]{1,0:T(8,128)}, f32[512,2048]{1,0:T(8,128)}) async-done(((f32[512,2048]{1,0:T(8,128)}, f32[512,2048]{1,0:T(8,128)}), (f32[512,2048]{1,0:T(8,128)}, f32[512,2048]{1,0:T(8,128)})) %all-reduce.9.cloned.1.call-update) | async-done | bytes 8388624 | tf_op jit(solution)/shard_map/psum | solution.py:126
  1052.9 4.8 multiply_bitcast_fusion
  1058.4 8.4 fusion.52
  1069.1 39.2 %reduce-scatter.10.cloned.1.call-done = f32[256,128]{1,0:T(8,128)} async-done(((f32[256,2048]{1,0:T(8,128)}), f32[256,128]{1,0:T(8,128)}) %reduce-scatter.10.cloned.1.call-update) | async-done | bytes 131088 | tf_op jit(solution)/shard_map/reduce_scatter | solution.py:166
  1110.2 5.6 add_convert_fusion
  1121.1 49.5 %reduce-scatter.16.cloned.1.call-done = f32[128,4]{1,0:T(8,128)} async-done(((f32[2048,4]{1,0:T(8,128)}), f32[128,4]{1,0:T(8,128)}) %reduce-scatter.16.cloned.1.call-update) | async-done | bytes 2064
  1172.1 80.0 %reduce-scatter.8.cloned.1.call-done = f32[3,128,256]{1,2,0:T(8,128)} async-done(((f32[3,2048,256]{1,2,0:T(8,128)}), f32[3,128,256]{1,2,0:T(8,128)}) %reduce-scatter.8.cloned.1.call-update) | async-done | bytes 393232 | tf_op jit(solution)/shard_map/reduce_scatter | solution.py:165
  1258.0 93.9 %reduce-scatter.12.cloned.1.call-done = f32[128,1024]{1,0:T(8,128)} async-done(((f32[2048,1024]{1,0:T(8,128)}), f32[128,1024]{1,0:T(8,128)}) %reduce-scatter.12.cloned.1.call-update) | async-done | bytes 524304 | tf_op jit(solution)/shard_map/reduce_scatter | solution.py:167
  (213 shorter events, 83.0 us)
Async XLA Ops:
  7.2 29.4 %copy-start.58 = (s32[1,16]{1,0:T(1,128)S(1)}, s32[1,16]{1,0:T(1,128)}, u32[]{:S(2)}) copy-start(s32[1,16]{1,0:T(1,128)} %param.25) | copy-start | bytes 196
  7.2 47.7 %all-gather.5.cloned.1.call-start = ((), (), s32[]{:S(2)}) async-start(), calls=%async_computation.5 | async-start | bytes 3342336 | tf_op jit(solution)/shard_map/all_gather | solution.py:86
  9.3 82.3 %all-gather.7.cloned.1.call-start = ((), (), s32[]{:S(2)}) async-start(), calls=%async_computation.6 | async-start | bytes 1114112 | tf_op jit(solution)/shard_map/all_gather | solution.py:87
  10.9 269.5 %all-reduce.5.cloned.1.call-start = ((), (), s32[]{:S(2)}) async-start(), calls=%async_computation.7 | async-start | bytes 8388608 | tf_op jit(solution)/shard_map/psum | solution.py:114
  95.5 223.8 %all-gather.9.cloned.1.call-start = ((), (), s32[]{:S(2)}) async-start(), calls=%async_computation.8 | async-start | bytes 4456448 | tf_op jit(solution)/shard_map/all_gather | solution.py:88
  97.4 331.5 %reduce-scatter.14.cloned.1.call-start = ((), (), s32[]{:S(2)}) async-start(), calls=%async_computation.14 | async-start | bytes 8912896 | tf_op jit(solution)/shard_map/reduce_scatter | solution.py:168
  332.8 146.2 %all-gather.11.cloned.1.call-start = ((), (), s32[]{:S(2)}) async-start(), calls=%async_computation.9 | async-start | bytes 4456448 | tf_op jit(solution)/shard_map/all_gather | solution.py:89
  432.3 243.8 %all-reduce.7.cloned.1.call-start = ((), (), s32[]{:S(2)}) async-start(), calls=%async_computation.10 | async-start | bytes 8388608 | tf_op jit(solution)/shard_map/psum | solution.py:127
  491.3 553.8 %all-reduce.9.cloned.1.call-start = ((), (), s32[]{:S(2)}) async-start(), calls=%async_computation.16 | async-start | bytes 16777216 | tf_op jit(solution)/shard_map/psum | solution.py:126
  703.5 404.8 %reduce-scatter.10.cloned.1.call-start = ((), (), s32[]{:S(2)}) async-start(), calls=%async_computation.12 | async-start | bytes 2228224 | tf_op jit(solution)/shard_map/reduce_scatter | solution.py:166
  707.2 341.1 %copy-start.37 = (f32[512]{0:T(512)S(1)}, f32[512]{0:T(512)}, u32[]{:S(2)}) copy-start(f32[512]{0:T(512)} %copy-done.36) | copy-start | bytes 6148
  707.2 341.1 %copy-start.23 = (f32[512]{0:T(512)S(1)}, f32[512]{0:T(512)}, u32[]{:S(2)}) copy-start(f32[512]{0:T(512)} %copy-done.22) | copy-start | bytes 6148
  707.2 341.1 %copy-start.41 = (f32[512]{0:T(512)S(1)}, f32[512]{0:T(512)}, u32[]{:S(2)}) copy-start(f32[512]{0:T(512)} %copy-done.40) | copy-start | bytes 6148
  707.3 463.3 %reduce-scatter.16.cloned.1.call-start = ((), (), s32[]{:S(2)}) async-start(), calls=%async_computation.15 | async-start | bytes 1114112
  1052.8 199.3 %reduce-scatter.8.cloned.1.call-start = ((), (), s32[]{:S(2)}) async-start(), calls=%async_computation.11 | async-start | bytes 6684672 | tf_op jit(solution)/shard_map/reduce_scatter | solution.py:165
  1057.7 294.2 %reduce-scatter.12.cloned.1.call-start = ((), (), s32[]{:S(2)}) async-start(), calls=%async_computation.13 | async-start | bytes 8912896 | tf_op jit(solution)/shard_map/reduce_scatter | solution.py:167
  1066.8 41.5 %copy-start.19 = (f32[256,128]{1,0:T(8,128)S(1)}, f32[256,128]{1,0:T(8,128)}, u32[]{:S(2)}) copy-start(f32[256,128]{1,0:T(8,128)} %param.27) | copy-start | bytes 393220
  1066.8 41.5 %copy-start.21 = (f32[256,128]{1,0:T(8,128)S(1)}, f32[256,128]{1,0:T(8,128)}, u32[]{:S(2)}) copy-start(f32[256,128]{1,0:T(8,128)} %param.34) | copy-start | bytes 393220
  1066.8 43.4 %copy-start.49 = (f32[512]{0:T(512)S(1)}, f32[512]{0:T(512)}, u32[]{:S(2)}) copy-start(f32[512]{0:T(512)} %get-tuple-element.138) | copy-start | bytes 6148
  1117.5 54.0 %copy-start.51 = (f32[4,128]{1,0:T(4,128)S(1)}, f32[4,128]{1,0:T(4,128)}, u32[]{:S(2)}) copy-start(f32[4,128]{1,0:T(4,128)} %param.30) | copy-start | bytes 6148
  1117.5 54.0 %copy-start.55 = (f32[4,128]{1,0:T(4,128)S(1)}, f32[4,128]{1,0:T(4,128)}, u32[]{:S(2)}) copy-start(f32[4,128]{1,0:T(4,128)} %param.40) | copy-start | bytes 6148
  1117.5 54.0 %copy-start.56 = (f32[4,128]{1,0:T(4,128)S(1)}, f32[4,128]{1,0:T(4,128)}, u32[]{:S(2)}) copy-start(f32[4,128]{1,0:T(4,128)} %param.39) | copy-start | bytes 6148
  1121.1 230.8 %copy-start.14 = (f32[128,1024]{1,0:T(8,128)S(1)}, f32[128,1024]{1,0:T(8,128)}, u32[]{:S(2)}) copy-start(f32[128,1024]{1,0:T(8,128)} %param.28) | copy-start | bytes 1572868
  1171.5 183.3 %copy-start.50 = (f32[4,128]{1,0:T(4,128)}, f32[4,128]{1,0:T(4,128)S(1)}, u32[]{:S(2)}) copy-start(f32[4,128]{1,0:T(4,128)S(1)} %copy.155) | copy-start | bytes 6148
  (50 other events, 273.0 us)
Sparse Core Ops, SparseCore 0:
  10.3 44.6 all-gather.4
  57.2 34.3 all-gather.6
  95.7 184.6 all-reduce.4
  282.5 36.8 all-gather.8
  332.9 96.0 reduce-scatter.13
  432.4 46.4 all-gather.10
  491.4 184.6 all-reduce.6
  703.6 341.4 all-reduce.8
  1048.1 60.1 reduce-scatter.9
  1110.5 60.0 reduce-scatter.15
  1173.1 78.9 reduce-scatter.7
  1255.1 96.7 reduce-scatter.11
where the time goes:
time: 1370 us; the launch traced here: 1360 us
  waiting for transfers between devices  1180 us (86%)
  matrix products  65.5 us (5%)
  other arithmetic  51.9 us (4%)
  local copies, waits for them, and re-layouts  27 us (2%)
  blocking collectives  21 us (2%)
  between operations  16.3 us (1%)
    psum x1, waiting for transfers between devices, per_device(): lax.psum(down_terms, 'tensor')  338 us
    psum x1, waiting for transfers between devices, per_device(): resid_one = inputs + lax.psum(attn_terms, 'tensor')  182 us
    psum x1, waiting for transfers between devices, per_device(): d_normed_two = lax.psum(entry_terms, 'tensor')  176 us
    reduce_scatter x1, waiting for transfers between devices, per_device(): lax.psum_scatter(local_down, 'dp', scatter_dimension=1, tiled=True)  95.8 us
    reduce_scatter x1, waiting for transfers between devices, per_device(): lax.psum_scatter(local_up, 'dp', scatter_dimension=0, tiled=True)  93.9 us
    reduce_scatter x1, waiting for transfers between devices, per_device(): lax.psum_scatter(local_qkv, 'dp', scatter_dimension=1, tiled=True)  80 us
    unnamed x13, waiting for transfers between devices  49.7 us
    all_gather x1, waiting for transfers between devices, per_device(): lax.all_gather(w_down.astype(jnp.bfloat16), 'dp', axis=1, tiled=True)  46.6 us
  transfers between devices with their start and end apart: 12, of which 12 were waited for; matrix products, arithmetic and copies ran while one was open for 5% of the time, Pallas kernels for 0%

commit v1 on v0

v1 whole, which is shorter than its diff:
```python
import functools

import jax
import jax.numpy as jnp
from jax import lax
from jax.experimental import pallas as pl
from jax.experimental.pallas import tpu as pltpu
from jax.sharding import PartitionSpec as P

HD = 128
STEP = 5
ROWS = 512
D = 2048
NEG_FILL = -1e30
BETA_ONE = 0.5
BETA_TWO = 0.5
ADAM_EPS = 1e-08
NORM_EPS = 1e-05
DECAY_RATE = 0.1
RATE_QKV = 0.02
RATE_OUT = 0.15
RATE_UP = 0.02
RATE_DOWN = 0.01
RATE_NORMS = 0.3
SCALE = HD ** (-0.5)
GELU_K = 0.7978845608028654
GELU_C = 0.044715

BF = jnp.bfloat16
F32 = jnp.float32
MESH = pl.DeviceIdType.MESH
NT = (((1,), (1,)), ((), ()))
TN = (((0,), (0,)), ((), ()))
NN = (((1,), (0,)), ((), ()))

SHARD = ((128, 256), (128, 256), (128, 256), (256, 128), (128, 1024), (1024, 128))
GATHER_X_FIRST = (True, True, False, False, True, False)
REDUCE_Y_FIRST = (True, True, False, False, False, True)
Q_, K_, V_, O_, U_, D_ = range(6)


def dot(a, b, dims=NN):
    return lax.dot_general(a, b, dims, preferred_element_type=F32)


def ds(start, size, mult=None):
    if not isinstance(start, int):
        start = pl.multiple_of(start, mult or size)
    return pl.ds(start, size)


class Counter:
    def __init__(self):
        self.n = 0

    def take(self, k=1):
        base = self.n
        self.n += k
        return base


def kernel(*refs):
    it = iter(refs)
    take = lambda n: [next(it) for _ in range(n)]
    tok_h, back_h, bias_h, nrm_in = take(4)
    wq_h, wo_h, wu_h, wd_h = take(4)
    bo_h, ig_h, gqkv_o, go_o, gu_o, gd_o, gn_o, r1u_h, r1d_h = take(9)
    wf_q, wf_o, wf_u, wf_d = take(4)
    own = take(6)
    gat = take(6)
    rcv1 = take(4) + [r1u_h, r1d_h]
    mid = take(6)
    rcv2 = take(6)
    (tile, tok, back, bias, a1, qkv, mixed, probs, a2, hid, dup, dhid, ps_a, ps_b) = take(14)
    rc = take(4)
    rz = take(4)
    (dt, r1, dr1, ybuf, dqkv, pb_s, ds_s, nst, nbuf, gains, ngrad, nrec, oblk_b, oblk_i) = take(14)
    ssem, rsem, lsem = take(3)

    d_at = lax.axis_index("dp")
    t_at = lax.axis_index("tensor")
    x = d_at // 4
    yl = (d_at // 2) % 2
    c = d_at % 2
    z = t_at // 2
    yh = t_at % 2
    y = yh * 2 + yl
    other = 1 - c

    def dev(px, py, pz, pc):
        return {"dp": (px * 2 + py % 2) * 2 + pc, "tensor": pz * 2 + py // 2}

    ns, nr, nl = Counter(), Counter(), Counter()
    pending = []

    def rcopy(src, dst, to, si, ri):
        return pltpu.make_async_remote_copy(
            src_ref=src, dst_ref=dst, send_sem=ssem.at[si], recv_sem=rsem.at[ri],
            device_id=to, device_id_type=MESH)

    def send(src, dst, to, ri, tag=""):
        cp = rcopy(src, dst, to, ns.take(), ri)
        cp.start()
        pending.append((tag, cp, None))

    def send_or_local(here, src, dst, to, ri, tag=""):
        cp = rcopy(src, dst, to, ns.take(), ri)
        away = jnp.logical_not(here)

        @pl.when(here)
        def _():
            pltpu.make_async_copy(src, dst, rsem.at[ri]).start()

        @pl.when(away)
        def _():
            cp.start()

        pending.append((tag, cp, away))

    def send_if(cond, src, dst, to, ri, tag=""):
        cp = rcopy(src, dst, to, ns.take(), ri)

        @pl.when(cond)
        def _():
            cp.start()

        pending.append((tag, cp, cond))

    def flush(tag=None):
        for item in pending[:]:
            kind, cp, cond = item
            if tag is None or kind == tag:
                pending.remove(item)
                if cond is None:
                    cp.wait_send()
                else:
                    pl.when(cond)(cp.wait_send)

    def got(dst, ri):
        rcopy(dst, dst, dev(x, y, z, other), 0, ri).wait_recv()

    loads = []

    def load(src, dst):
        cp = pltpu.make_async_copy(src, dst, lsem.at[nl.take()])
        cp.start()
        loads.append(cp)
        return cp

    ld_q = load(wq_h, wf_q)
    ld_o = load(wo_h, wf_o)
    ld_u = load(wu_h, wf_u)
    ld_d = load(wd_h, wf_d)

    yp = yh * 2 + (1 - yl)
    peers = [dev(x, y, z, other)]
    for k in (1, 2, 3):
        for cc in (0, 1):
            peers.append(dev((x + k) % 4, y, z, cc))
            peers.append(dev(x, (y + k) % 4, z, cc))
            peers.append(dev(x, y, (z + k) % 4, cc))
            peers.append(dev((x + k) % 4, yp, z, cc))
    barrier = pltpu.get_barrier_semaphore()
    for peer in peers:
        pl.semaphore_signal(barrier, inc=1, device_id=peer, device_id_type=MESH)
    nst[0:4, :] = nrm_in[...].astype(BF).astype(F32)
    nst[4:8, :] = jnp.zeros((4, 128), F32)
    ld_q.wait()
    for j in range(3):
        own[j][...] = wf_q[j].astype(BF)
    ld_o.wait()
    own[O_][...] = wf_o[...].astype(BF)
    pl.semaphore_wait(barrier, len(peers))

    tok_r = nr.take(3)
    group_in = ((tok_h, tok), (bias_h, bias), (back_h, back))
    home = c == yh

    def share(i):
        src, dst = group_in[i]
        send_if(home, src, dst, dev(x, y, z, other), tok_r + i)

        @pl.when(home)
        def _():
            pltpu.make_async_copy(src, dst, rsem.at[tok_r + i]).start()

    norm_r = nr.take(16)
    for dx in range(4):
        for dl in (0, 1):
            for dc in (0, 1):
                if dx or dl or dc:
                    to = dev((x + dx) % 4, yh * 2 + (yl + dl) % 2, z, (c + dc) % 2)
                    send(nst, nbuf.at[d_at], to, norm_r + d_at)

    g1_r = [nr.take(8) for _ in range(6)]
    g2_r = [nr.take(4) for _ in range(6)]

    def gather_one(k):
        for j in range(4):
            if GATHER_X_FIRST[k]:
                px = (x + j) % 4
                slot, to = g1_r[k] + x * 2 + c, dev(px, y, z, yh)
            else:
                py = (y + j) % 4
                slot, to = g1_r[k] + yl * 2 + c, dev(x, py, z, yh)
            dst = gat[k].at[x, yl, c]
            if j == 0:
                send_or_local(home, own[k], dst, to, slot, "gather")
            else:
                send(own[k], dst, to, slot, "gather")

    r_at = (y + 4 - 2 * c) % 4

    def gather_two(k):
        if GATHER_X_FIRST[k]:
            @pl.when(home)
            def _():
                for sx in range(4):
                    for sc in range(2):
                        got(gat[k].at[sx, yl, sc], g1_r[k] + sx * 2 + sc)

            part = gat[k].at[:, yl]
            for step in (1, 3):
                send_if(home, part, part, dev(x, (y + step) % 4, z, c), g2_r[k], "gather")
        else:
            for sl in range(2):
                for sc in range(2):
                    got(gat[k].at[x, sl, sc], g1_r[k] + sl * 2 + sc)
            part = gat[k].at[x]
            send(part, part, dev((x + 1) % 4, y, z, c), g2_r[k], "gather")
            send(part, part, dev((x + 3) % 4, y, z, c), g2_r[k] + 1, "gather")

    def gather_three(k):
        if GATHER_X_FIRST[k]:
            src_l = 1 - r_at % 2
            got(gat[k].at[:, src_l], g2_r[k])
            half = jnp.where((r_at == 0) | (r_at == 3), 1, 0)
            part = gat[k].at[pl.ds(2 * half, 2), src_l]
            to = dev(x, (2 * c + 3 - r_at % 2) % 4, z, c)
            send(part, part, to, g2_r[k] + 1 + half, "gather")
        else:
            xm, xp = (x + 3) % 4, (x + 1) % 4
            got(gat[k].at[xm], g2_r[k])
            part = gat[k].at[xm, 0]
            send(part, part, dev(xp, y, z, c), g2_r[k] + 2, "gather")
            got(gat[k].at[xp], g2_r[k] + 1)
            part = gat[k].at[xp, 1]
            send(part, part, dev(xm, y, z, c), g2_r[k] + 3, "gather")

    def gather_end(k):
        if GATHER_X_FIRST[k]:
            @pl.when(r_at >= 2)
            def _():
                for half in range(2):
                    got(gat[k].at[pl.ds(2 * half, 2), r_at % 2], g2_r[k] + 1 + half)
        else:
            x2 = (x + 2) % 4
            got(gat[k].at[x2, 0], g2_r[k] + 2)
            got(gat[k].at[x2, 1], g2_r[k] + 3)

    share(0)
    for k in (Q_, K_, V_, O_):
        gather_one(k)
    ld_u.wait()

    @pl.loop(0, 8)
    def _(i):
        own[U_][ds(i * 16, 16), :] = wf_u[ds(i * 16, 16), :].astype(BF)

    ld_d.wait()

    @pl.loop(0, 8)
    def _(i):
        own[D_][ds(i * 128, 128), :] = wf_d[ds(i * 128, 128), :].astype(BF)

    for dx in range(4):
        for dl in (0, 1):
            for dc in (0, 1):
                if dx or dl or dc:
                    sd = (((x + dx) % 4) * 2 + (yl + dl) % 2) * 2 + (c + dc) % 2
                    got(nbuf.at[sd], norm_r + sd)
    nbuf[d_at] = nst[...]
    for i in range(16):
        gains[:, i * 128:(i + 1) * 128] = nbuf[i]

    got(tok, tok_r)

    @pl.loop(0, ROWS // 32)
    def _(i):
        rows = ds(i * 32, 32)
        v = tok[rows, :].astype(F32)
        cen = v - jnp.mean(v, axis=-1, keepdims=True)
        var = jnp.mean(cen * cen, axis=-1, keepdims=True)
        a1[rows, :] = (cen * lax.rsqrt(var + NORM_EPS) * gains[0:1, :] + gains[1:2, :]).astype(BF)

    for k in (Q_, K_, V_, O_):
        gather_two(k)
    share(1)
    share(2)
    gather_one(U_)
    gather_one(D_)
    for k in (Q_, K_, V_, O_):
        gather_three(k)

    def project(j):
        gather_end(j)

        @pl.loop(0, 2)
        def _(i):
            rows = ds(i * 256, 256)
            v = dot(a1[rows, :], gat[j][...].reshape(D, 256))
            if j == Q_:
                v = v * SCALE
            qkv[j, rows, :] = v.astype(BF)

    project(Q_)
    project(K_)
    project(V_)
    gather_two(U_)
    gather_two(D_)
    got(bias, tok_r + 1)

    for h in range(2):
        cols = slice(h * HD, (h + 1) * HD)

        @pl.loop(0, 4)
        def _(i):
            rows = ds(i * 128, 128)
            s = dot(qkv[0, rows, cols], qkv[1, :, cols], NT) + bias[rows, :].astype(F32)
            w = jnp.exp(s - jnp.max(s, axis=-1, keepdims=True))
            p = w / jnp.sum(w, axis=-1, keepdims=True)
            probs[h, rows, :] = p
            mixed[rows, cols] = dot(p.astype(BF), qkv[2, :, cols]).astype(BF)

    my_row = c * 256 + z * 64
    rc_r = [nr.take() for _ in range(4)]
    rz_r = [nr.take(3) for _ in range(4)]

    def sum_start(k, ps, compute):
        lo = other * 256
        compute(lo)
        half = ps.at[ds(lo, 256), :]
        send(half, rc[k], dev(x, y, z, other), rc_r[k], f"sum{k}")
        compute(c * 256)

    def sum_middle(k, ps):
        got(rc[k], rc_r[k])
        for dz in (2, 1, 3, 0):
            pz = (z + dz) % 4
            base = c * 256 + pz * 64

            @pl.loop(0, 4)
            def _(i):
                rows = ds(base + i * 16, 16)
                from_other = rc[k][ds(pz * 64 + i * 16, 16), :].astype(F32)
                ps[rows, :] = (ps[rows, :].astype(F32) + from_other).astype(BF)

            if dz:
                send(ps.at[ds(base, 64), :], rz[k].at[dz - 1], dev(x, y, pz, c), rz_r[k] + dz - 1, f"sum{k}")

    def sum_wait(k):
        for dz in (1, 3, 2):
            got(rz[k].at[dz - 1], rz_r[k] + dz - 1)

    def sum_rows(k, ps, i):
        rows = ds(i * 16, 16)
        v = ps[ds(my_row + i * 16, 16), :].astype(F32)
        for j in range(3):
            v = v + rz[k][j, rows, :].astype(F32)
        return v

    ag_r = [nr.take(3) for _ in range(2)]
    ac_r = [nr.take(4) for _ in range(2)]

    def spread_start(k, buf):
        part = buf.at[ds(my_row, 64), :]
        for dz in (2, 1, 3):
            send(part, part, dev(x, y, (z + dz) % 4, c), ag_r[k] + dz - 1)
        send(part, part, dev(x, y, z, other), ac_r[k] + z)

    def spread_pass(k, buf):
        for dz in (1, 3, 2):
            sz = (z + 4 - dz) % 4
            part = buf.at[ds(c * 256 + sz * 64, 64), :]
            got(part, ag_r[k] + dz - 1)
            send(part, part, dev(x, y, z, other), ac_r[k] + sz)

    def spread_end(k, buf):
        for sz in range(4):
            got(buf.at[ds(other * 256 + sz * 64, 64), :], ac_r[k] + sz)

    def attn_out(lo):
        gather_end_once(O_)

        @pl.loop(0, 4)
        def _(i):
            cols = [gat[O_][i, a, b] for a in range(2) for b in range(2)]
            v = dot(mixed[ds(lo, 256), :], jnp.concatenate(cols, axis=1))
            ps_a[ds(lo, 256), ds(i * 512, 512)] = v.astype(BF)

    done = set()

    def gather_end_once(k):
        if k not in done:
            done.add(k)
            gather_end(k)

    sum_start(0, ps_a, attn_out)
    sum_middle(0, ps_a)
    gather_three(U_)
    gather_three(D_)
    sum_wait(0)

    @pl.loop(0, 4)
    def _(i):
        rows = ds(i * 16, 16)
        v = tok[ds(my_row + i * 16, 16), :].astype(F32) + sum_rows(0, ps_a, i)
        r1[rows, :] = v
        cen = v - jnp.mean(v, axis=-1, keepdims=True)
        var = jnp.mean(cen * cen, axis=-1, keepdims=True)
        n = cen * lax.rsqrt(var + NORM_EPS) * gains[2:3, :] + gains[3:4, :]
        a2[ds(my_row + i * 16, 16), :] = n.astype(BF)

    spread_start(0, a2)
    spread_pass(0, a2)

    got(back, tok_r + 2)
    gather_end(D_)

    @pl.loop(0, 4)
    def _(i):
        hrows = ds(i * 256, 256)
        w = jnp.concatenate([gat[D_][a, b, e, hrows, :] for a in range(4) for b in range(2) for e in range(2)], axis=1)
        dhid[:, hrows] = dot(back[...], w, NT)

    gather_end(U_)
    spread_end(0, a2)

    @pl.loop(0, 4)
    def _(i):
        cols = ds(i * 256, 256)
        u = dot(a2[...], gat[U_][:, :, :, :, cols].reshape(D, 256))
        th = jnp.tanh(GELU_K * (u + GELU_C * u * u * u))
        hid[:, cols] = (0.5 * u * (1.0 + th)).astype(BF)
        slope = 0.5 * (1.0 + th) + 0.5 * u * (1.0 - th * th) * (GELU_K * (1.0 + 3.0 * GELU_C * u * u))
        dup[:, cols] = (dhid[:, cols] * slope).astype(BF)

    def entry(lo):
        @pl.loop(0, 4)
        def _(i):
            w = gat[U_][i].reshape(512, 1024)
            ps_a[ds(lo, 256), ds(i * 512, 512)] = dot(dup[ds(lo, 256), :], w, NT).astype(BF)

    def down(lo):
        @pl.loop(0, 4)
        def _(i):
            w = jnp.concatenate([gat[D_][i, a, b] for a in range(2) for b in range(2)], axis=1)
            ps_b[ds(lo, 256), ds(i * 512, 512)] = dot(hid[ds(lo, 256), :], w).astype(BF)

    flush("sum0")
    sum_start(1, ps_a, entry)
    sum_middle(1, ps_a)
    sum_start(2, ps_b, down)

    s1_r = [nr.take(4) for _ in range(6)]
    s2_r = [nr.take(4) for _ in range(6)]

    def scatter_one(k):
        if REDUCE_Y_FIRST[k]:
            for tl in range(2):
                for tc in range(2):
                    here = home & (yl == tl) & (c == tc)
                    src, dst = gat[k].at[:, tl, tc], rcv1[k].at[y]
                    send_or_local(here, src, dst, dev(x, 2 * c + tl, z, tc), s1_r[k] + y)
        else:
            for dx in (2, 1, 3):
                px = (x + dx) % 4
                send(gat[k].at[px], rcv1[k].at[dx - 1], dev(px, y, z, c), s1_r[k] + dx - 1)

    def add_up(parts, out, shape, scale=None):
        step = 16384 // shape[1]

        @pl.loop(0, shape[0] // step)
        def _(i):
            rows = ds(i * step, step)
            v = parts[0][rows, :].astype(F32)
            for p in parts[1:]:
                v = v + p[rows, :].astype(F32)
            if scale is not None:
                v = v * scale
            out[rows, :] = v.astype(out.dtype)

    def scatter_two(k):
        in_hbm = k in (U_, D_)
        if REDUCE_Y_FIRST[k]:
            for sy in range(4):
                got(rcv1[k].at[sy], s1_r[k] + sy)
            places = [(x + dx) % 4 for dx in (2, 1, 3, 0)]
            pick = [lambda p, sy=sy: rcv1[k].at[sy, p] for sy in range(4)]
        else:
            for j in range(3):
                got(rcv1[k].at[j], s1_r[k] + j)
            places = [(a, b) for a in range(2) for b in range(2)]
            pick = [lambda p, j=j: rcv1[k].at[j, p[0], p[1]] for j in range(3)]
        copies = []
        if in_hbm:
            base = nl.take(8)

            def fetch(i):
                cps = []
                for j, f in enumerate(pick):
                    cp = pltpu.make_async_copy(
                        f(places[i]), tiles(k, i % 2, j), lsem.at[base + (i % 2) * 4 + j])
                    cp.start()
                    cps.append(cp)
                return cps

            copies = fetch(0)
        for i, place in enumerate(places):
            if in_hbm:
                for cp in copies:
                    cp.wait()
                parts = [tiles(k, i % 2, j) for j in range(len(pick))]
                if i + 1 < len(places):
                    copies = fetch(i + 1)
            else:
                parts = [f(place) for f in pick]
            if REDUCE_Y_FIRST[k]:
                out = mid[k].at[place]
                add_up(parts, out, SHARD[k])
                to = dev(place, y, z, c)
                if i == 3:
                    pltpu.make_async_copy(out, rcv2[k].at[x], rsem.at[s2_r[k] + x]).start()
                else:
                    send(out, rcv2[k].at[x], to, s2_r[k] + x)
            else:
                out = mid[k].at[place[0], place[1]]
                add_up(parts + [gat[k].at[x, place[0], place[1]]], out, SHARD[k])
                here = home & (yl == place[0]) & (c == place[1])
                send_or_local(here, out, rcv2[k].at[y], dev(x, 2 * c + place[0], z, place[1]), s2_r[k] + y)

    def tiles(k, slot, j):
        return (tile_u if k == U_ else tile_d).at[slot, j]

    tile_u, tile_d = tile

    def scatter_end(k, out, scale=None):
        for j in range(4):
            got(rcv2[k].at[j], s2_r[k] + j)
        add_up([rcv2[k].at[j] for j in range(4)], out, SHARD[k], scale)

    flush("gather")

    @pl.loop(0, 8)
    def _(i):
        v = dot(hid[...], back[:, ds(i * 256, 256)], TN).astype(BF)
        a, b = i // 2, i % 2
        gat[D_][a, b, 0] = v[:, :128]
        gat[D_][a, b, 1] = v[:, 128:]

    scatter_one(D_)
    sum_middle(2, ps_b)

    @pl.loop(0, 8)
    def _(i):
        a, b = i // 2, i % 2
        v = dot(a2[:, ds(i * 256, 256)], dup[...], TN).astype(BF)
        gat[U_][a, b, 0] = v[:128]
        gat[U_][a, b, 1] = v[128:]

    scatter_one(U_)

    def norm_back(v, dy, gain):
        cen = v - jnp.mean(v, axis=-1, keepdims=True)
        rs = lax.rsqrt(jnp.mean(cen * cen, axis=-1, keepdims=True) + NORM_EPS)
        xh = cen * rs
        e = dy * gain
        dv = rs * (e - jnp.mean(e, axis=-1, keepdims=True) - xh * jnp.mean(e * xh, axis=-1, keepdims=True))
        return dv, jnp.sum(dy * xh, axis=0, keepdims=True), jnp.sum(dy, axis=0, keepdims=True)

    ngrad[...] = jnp.zeros_like(ngrad)
    sum_wait(1)

    @pl.loop(0, 4)
    def _(i):
        rows = ds(i * 16, 16)
        mine = ds(my_row + i * 16, 16)
        dv, dg, db = norm_back(r1[rows, :], sum_rows(1, ps_a, i), gains[2:3, :])
        v = back[mine, :].astype(F32) + dv
        dr1[rows, :] = v
        dt[mine, :] = v.astype(BF)
        ngrad[2:3, :] += dg
        ngrad[3:4, :] += db

    spread_start(1, dt)

    o1_r = [nr.take(8) for _ in range(2)]

    def out_start(k, blk, out):
        part = out.at[ds(my_row, 64), :]
        for dz in (2, 1, 3):
            send(blk, part, dev(x, y, (z + dz) % 4, yh), o1_r[k] + z * 2 + c)
        send_or_local(home, blk, part, dev(x, y, z, yh), o1_r[k] + z * 2 + c)
        y2 = (y + 2) % 4
        send(blk, part, dev(x, y2, z, yh), o1_r[k] + z * 2 + c)

    def out_pass(k, out):
        away = jnp.logical_not(home)
        for sc in range(2):
            part = out.at[ds(sc * 256 + z * 64, 64), :]

            @pl.when(away)
            def _():
                got(part, o1_r[k] + z * 2 + sc)

            for dz in (2, 1, 3):
                send_if(away, part, part, dev(x, y, (z + dz) % 4, c), o1_r[k] + z * 2 + sc)

    def out_end(k, out):
        away = jnp.logical_not(home)
        for sc in range(2):
            for dz in range(4):
                sz = (z + dz) % 4

                def wait_it():
                    got(out.at[ds(sc * 256 + sz * 64, 64), :], o1_r[k] + sz * 2 + sc)

                if dz == 0:
                    pl.when(home)(wait_it)
                else:
                    wait_it()

    spread_pass(1, dt)
    sum_wait(2)

    @pl.loop(0, 4)
    def _(i):
        rows = ds(i * 16, 16)
        oblk_b[rows, :] = (r1[rows, :] + sum_rows(2, ps_b, i)).astype(BF)

    spread_end(1, dt)

    @pl.loop(0, 2)
    def _(i):
        rows = ds(i * 256, 256)
        w = jnp.concatenate([gat[O_][a, b, e] for a in range(4) for b in range(2) for e in range(2)], axis=1)
        ybuf[rows, :] = dot(dt[rows, :], w, NT).astype(BF)

    for h in range(2):
        cols = slice(h * HD, (h + 1) * HD)

        @pl.loop(0, 4)
        def _(i):
            rows = ds(i * 128, 128)
            p = probs[h, rows, :]
            pb_s[rows, :] = p.astype(BF)
            dp = dot(ybuf[rows, cols], qkv[2, :, cols], NT)
            d_s = (p * (dp - jnp.sum(p * dp, axis=-1, keepdims=True))).astype(BF)
            ds_s[rows, :] = d_s
            dqkv[rows, cols] = dot(d_s, qkv[1, :, cols]).astype(BF)

        dqkv[:, 256 + h * HD:256 + (h + 1) * HD] = dot(ds_s[...], qkv[0, :, cols], TN).astype(BF)
        dqkv[:, 512 + h * HD:512 + (h + 1) * HD] = dot(pb_s[...], ybuf[:, cols], TN).astype(BF)

    def into_norm(lo):
        @pl.loop(0, 4)
        def _(i):
            ws = [gat[j][i].reshape(512, 256) for j in range(3)]
            v = dot(dqkv[ds(lo, 256), 0:256], ws[0], NT) * SCALE
            v = v + dot(dqkv[ds(lo, 256), 256:512], ws[1], NT)
            v = v + dot(dqkv[ds(lo, 256), 512:768], ws[2], NT)
            ps_a[ds(lo, 256), ds(i * 512, 512)] = v.astype(BF)

    flush("sum1")
    sum_start(3, ps_a, into_norm)
    sum_middle(3, ps_a)

    @pl.loop(0, 16)
    def _(i):
        a, b, e = i // 4, (i // 2) % 2, i % 2
        v = dot(a1[:, ds(i * 128, 128)], dqkv[...], TN)
        for j in range(3):
            w = v[:, j * 256:(j + 1) * 256]
            gat[j][a, b, e] = (w * SCALE if j == 0 else w).astype(BF)

    for k in (Q_, K_, V_):
        scatter_one(k)

    @pl.loop(0, 8)
    def _(i):
        v = dot(mixed[...], dt[:, ds(i * 256, 256)], TN).astype(BF)
        gat[O_][i // 2, i % 2, 0] = v[:, :128]
        gat[O_][i // 2, i % 2, 1] = v[:, 128:]

    scatter_one(O_)
    scatter_two(D_)
    scatter_two(U_)
    out_start(0, oblk_b, bo_h)

    sum_wait(3)

    @pl.loop(0, 4)
    def _(i):
        rows = ds(i * 16, 16)
        v = tok[ds(my_row + i * 16, 16), :].astype(F32)
        dv, dg, db = norm_back(v, sum_rows(3, ps_a, i), gains[0:1, :])
        oblk_i[rows, :] = (dr1[rows, :] + dv).astype(BF)
        ngrad[0:1, :] += dg
        ngrad[1:2, :] += db

    out_start(1, oblk_i, ig_h)

    n_r = [nr.take(7), nr.take(3), nr.take(3)]

    def norm_sum(stage, targets, base):
        for j, to in enumerate(targets):
            send(ngrad, nrec.at[base + j], to, n_r[stage] + j, "norm")
        flush("norm")
        for j in range(len(targets)):
            got(nrec.at[base + j], n_r[stage] + j)
        v = ngrad[...]
        for j in range(len(targets)):
            v = v + nrec[base + j]
        ngrad[...] = v

    norm_sum(0, [dev(x, y, (z + dz) % 4, (c + dc) % 2) for dz in range(4) for dc in range(2) if dz or dc], 0)
    for k in (Q_, K_, V_, O_):
        scatter_two(k)
    out_pass(0, bo_h)
    out_pass(1, ig_h)
    norm_sum(1, [dev((x + k) % 4, y, z, c) for k in (1, 2, 3)], 7)
    norm_sum(2, [dev(x, (y + k) % 4, z, c) for k in (1, 2, 3)], 10)
    gn_o[...] = ngrad[...]

    scatter_end(D_, gd_o)
    scatter_end(U_, gu_o)
    for j in range(3):
        scatter_end(j, gqkv_o.at[j])
    scatter_end(O_, go_o)
    out_end(0, bo_h)
    out_end(1, ig_h)
    flush()


def run_layer(tokens, back_rows, bias, norms, w_qkv, w_out, w_up, w_down):
    hbm = pl.BlockSpec(memory_space=pltpu.HBM)
    vmem = pl.BlockSpec(memory_space=pltpu.VMEM)
    shards = [(4, 2, 2) + s for s in SHARD]
    rcv1 = [(4, 4) + s if REDUCE_Y_FIRST[k] else (3, 2, 2) + s for k, s in enumerate(SHARD)]
    mid = [(4,) + s if REDUCE_Y_FIRST[k] else (2, 2) + s for k, s in enumerate(SHARD)]
    big = lambda s, t=BF: pltpu.VMEM(s, t)
    scratch = [big((3, 128, 256), F32), big((256, 128), F32), big((128, 1024), F32), big((1024, 128), F32)]
    scratch += [big(s) for s in SHARD]
    scratch += [big(s) for s in shards]
    scratch += [big(rcv1[k]) for k in (Q_, K_, V_, O_)]
    scratch += [big(s) for s in mid]
    scratch += [big((4,) + s) for s in SHARD]
    scratch += [
        [big((2, 3, 128, 1024)), big((2, 4, 1024, 128))],
        big((ROWS, D)), big((ROWS, D)), big((ROWS, ROWS)), big((ROWS, D)), big((3, ROWS, 256)),
        big((ROWS, 256)), big((2, ROWS, ROWS), F32), big((ROWS, D)), big((ROWS, 1024)), big((ROWS, 1024)),
        big((ROWS, 1024), F32), big((ROWS, D)), big((ROWS, D)),
    ]
    scratch += [big((256, D))] * 4
    scratch += [big((3, 64, D))] * 4
    scratch += [
        big((ROWS, D)), big((64, D), F32), big((64, D), F32), big((ROWS, 256)), big((ROWS, 768)),
        big((ROWS, ROWS)), big((ROWS, ROWS)), big((8, 128), F32), big((16, 8, 128), F32), big((8, D), F32),
        big((8, D), F32), big((13, 8, D), F32), big((64, D)), big((64, D)),
    ]
    scratch += [pltpu.SemaphoreType.DMA((260,)), pltpu.SemaphoreType.DMA((260,)), pltpu.SemaphoreType.DMA((32,))]
    out_shape = [
        jax.ShapeDtypeStruct((ROWS, D), BF), jax.ShapeDtypeStruct((ROWS, D), BF),
        jax.ShapeDtypeStruct((3, 128, 256), F32), jax.ShapeDtypeStruct((256, 128), F32),
        jax.ShapeDtypeStruct((128, 1024), F32), jax.ShapeDtypeStruct((1024, 128), F32),
        jax.ShapeDtypeStruct((8, D), F32),
        jax.ShapeDtypeStruct(rcv1[U_], BF), jax.ShapeDtypeStruct(rcv1[D_], BF),
    ]
    return pl.pallas_call(
        kernel,
        out_shape=out_shape,
        in_specs=[hbm, hbm, hbm, vmem, hbm, hbm, hbm, hbm],
        out_specs=[hbm, hbm, vmem, vmem, vmem, vmem, vmem, hbm, hbm],
        scratch_shapes=scratch,
        compiler_params=pltpu.CompilerParams(
            collective_id=0, has_side_effects=True, vmem_limit_bytes=63 * 2**20),
    )(tokens, back_rows, bias, norms, w_qkv, w_out, w_up, w_down)[:7]


def layout(group_size, prefix_len, slot_lens, length):
    slot_count = slot_lens.shape[0]
    slot_live = jnp.arange(slot_count, dtype=jnp.int32) < group_size
    counted = jnp.where(slot_live, slot_lens, 0)
    seg_ends = prefix_len + jnp.cumsum(counted)
    position = jnp.arange(length, dtype=jnp.int32)
    segment = jnp.sum((position[:, None] >= seg_ends[None, :]).astype(jnp.int32), axis=1)
    segment = jnp.where(position < prefix_len, -1, segment)
    valid_rows = position < seg_ends[slot_count - 1]
    linked = (segment[:, None] == segment[None, :]) | (segment[None, :] < 0)
    causal = position[None, :] <= position[:, None]
    allowed = linked & causal & valid_rows[:, None] & valid_rows[None, :]
    allowed = allowed | (position[:, None] == position[None, :])
    return (allowed, valid_rows)


def adamw(weight, grad_in, first_old, second_old, step_rate, weight_decay):
    first_new = BETA_ONE * first_old + (1.0 - BETA_ONE) * grad_in
    second_new = BETA_TWO * second_old + (1.0 - BETA_TWO) * grad_in * grad_in
    corr_one = 1.0 - BETA_ONE**STEP
    corr_two = 1.0 - BETA_TWO**STEP
    step_dir = first_new / corr_one / (jnp.sqrt(second_new / corr_two) + ADAM_EPS)
    weight_new = weight - step_rate * (step_dir + weight_decay * weight)
    return (grad_in, first_new, second_new, weight_new, weight_new.astype(jnp.bfloat16))


def per_device(
    tokens, cotangent, group_sizes, prefix_lens, solution_lens,
    w_qkv, w_out, w_up, w_down, norms,
    first_qkv, second_qkv, first_out, second_out,
    first_up, second_up, first_down, second_down, first_norms, second_norms,
):
    length = tokens.shape[0]
    allowed, valid_rows = layout(group_sizes[0], prefix_lens[0], solution_lens[0], length)
    bias = jnp.where(allowed, 0.0, NEG_FILL).astype(BF)
    back_rows = jnp.where(valid_rows[:, None], cotangent, jnp.zeros_like(cotangent))
    block_out, input_grad, grad_qkv, grad_out, grad_up, grad_down, grad_norms = run_layer(
        tokens, back_rows, bias, norms, w_qkv, w_out, w_up, w_down)
    at = lax.axis_index("dp") * 128
    grad_norm_rows = lax.dynamic_slice(grad_norms, (0, at), (4, 128))
    qkv_res = adamw(w_qkv, grad_qkv, first_qkv, second_qkv, RATE_QKV, DECAY_RATE)
    out_res = adamw(w_out, grad_out, first_out, second_out, RATE_OUT, DECAY_RATE)
    up_res = adamw(w_up, grad_up, first_up, second_up, RATE_UP, DECAY_RATE)
    down_res = adamw(w_down, grad_down, first_down, second_down, RATE_DOWN, DECAY_RATE)
    norm_res = adamw(norms, grad_norm_rows, first_norms, second_norms, RATE_NORMS, 0.0)
    return (block_out, input_grad.astype(F32), *qkv_res, *out_res, *up_res, *down_res, *norm_res)


def solution(mesh):
    row, mat = P("dp", None), P("tensor", "dp")
    qkv, up, nrm = P(None, "dp", "tensor"), P("dp", "tensor"), P(None, "dp")
    return jax.shard_map(
        per_device,
        mesh=mesh,
        in_specs=(row, row, P("dp"), P("dp"), row, qkv, mat, up, mat, nrm,
                  qkv, qkv, mat, mat, up, up, mat, mat, nrm, nrm),
        out_specs=(row, row) + (qkv,) * 5 + (mat,) * 5 + (up,) * 5 + (mat,) * 5 + (nrm,) * 5,
        check_vma=False,
    )
```

time: 1370 us -> 251 us (0.18)
  waiting for transfers between devices: 1180 us -> 0 us
  Pallas kernels: 0 us -> 227 us
  matrix products: 65.5 us -> 0 us
  other arithmetic: 51.9 us -> 16.2 us
  local copies, waits for them, and re-layouts: 27 us -> 5.21 us
  blocking collectives: 21 us -> 0 us
  between operations: 16.3 us -> 2.15 us
    psum x3 -> x0, waiting for transfers between devices: 696 us -> none  [the longest x1 338 us: per_device(): lax.psum(down_terms, 'tensor')]
    reduce_scatter x4 -> x0, waiting for transfers between devices: 309 us -> none  [the longest x1 95.8 us: per_device(): lax.psum_scatter(local_down, 'dp', scatter_dimension=1, tiled=True)]
    pallas_call x0 -> x1, Pallas kernels: none -> 227 us  [run_layer(): pl.pallas_call(kernel, out_shape=out_shape, in_specs=[hbm, hbm, hbm, vmem...]
    all_gather x4 -> x0, waiting for transfers between devices: 125 us -> none  [the longest x1 46.6 us: per_device(): lax.all_gather(w_down.astype(jnp.bfloat16), 'dp', axis=1, tiled=True)]
    dot_general x18 -> x0, matrix products: 65.5 us -> none  [the longest x1 8.36 us: per_device(): jnp.einsum('sd,sf->df', normed_two, d_up, preferred_element_type=jnp.floa...]
    unnamed x13 -> x0, waiting for transfers between devices: 49.7 us -> none
    all_gather x1 -> x0, blocking collectives: 21 us -> none  [per_device(): lax.all_gather(norms.astype(jnp.bfloat16), 'dp', axis=1, tiled=True)]
    reduce_sum x9 -> x0, other arithmetic: 18.8 us -> none  [the longest x3 11.3 us: layer_norm(): return centered * lax.rsqrt(spread + NORM_EPS) * norm_gain + norm_shift]
  transfers between devices with their start and end apart: 12 -> 0, of which waited for: 12 -> 0; matrix products, arithmetic and copies ran while one was open for 5% -> 0% of each run, Pallas kernels for 0% -> 0%
where the time goes in v1:
time: 251 us; the launch traced here: 250 us
  Pallas kernels  227 us (90%)
  other arithmetic  16.2 us (6%)
  local copies, waits for them, and re-layouts  5.21 us (2%)
    pallas_call x1, Pallas kernels, run_layer(): pl.pallas_call(kernel, out_shape=out_shape, in_specs=[hbm, hbm, hbm, vmem...  227 us
    convert_element_type x5, other arithmetic, adamw(): weight_new.astype(jnp.bfloat16)  7.91 us

profile of v1, /device:TPU:1, one launch (start us, length us, event | category | flops | bytes accessed | tf_op | source)
XLA Modules:
  0.0 250.2 jit_solution(5659994623758690779)
XLA Ops:
  2.0 0.7 compare_select_fusion
  2.6 0.1 copy.49
  2.7 0.1 fusion.21
  2.9 0.1 convert_reduce_fusion
  3.0 0.5 slice.5
  3.5 0.7 broadcast_compare_fusion
  4.1 1.1 select_convert_fusion.refs_2_
  5.2 3.1 %broadcast_select_fusion.refs_1_ = bf16[512,2048]{1,0:T(8,128)(2,1)} fusion(bf16[512,2048]{1,0:T(8,128)(2,1)} %param.21, pred[512]{0:T(512)(128)(4,1)S(1)} %get-tuple-element.66), kind=kLoop, calls=%fused_computation | loop fusion | flops 1048576 | bytes 4194816 | tf_op jit(solution)/shard_map/jit(_where)/select_n | solution.py:825
  8.4 226.7 %shard_map.403 = (bf16[512,2048]{1,0:T(8,128)(2,1)}, bf16[512,2048]{1,0:T(8,128)(2,1)}, f32[3,128,256]{2,1,0:T(8,128)}, f32[256,128]{1,0:T(8,128)}, f32[128,1024...) custom-call(bf16[512,2048]{1,0:T(8,128)(2,1)} %refs_0_.1, ...), custom_call_target="tpu_custom_call" | custom-call | tf_op jit(solution)/shard_map/pallas_call | solution.py:779
  235.0 0.0 copy-start.2
  235.1 0.0 copy-start.9
  235.1 1.4 fusion.10
  236.5 2.9 %fusion.14 = (bf16[128,1024]{1,0:T(8,128)(2,1)}, f32[128,1024]{1,0:T(8,128)}, f32[128,1024]{1,0:T(8,128)}, f32[128,1024]{1,0:T(8,128)}) fusion(f32[128,1024]{1,0:T(8,128)S(1)} %copy-done.1, f32[128,1024]{1,0:T(8,128)} %get-tuple-element.106, f32[128,1024]{1,0:T(8,128)} %param.35, f32[128,1024]{1,0:T(8,128)} %param.34), kind=kLoop, calls=%fused_computation.39 | loop fusion | flops 1966080 | bytes 3932160 | tf_op jit(solution)/shard_map/convert_element_type | solution.py:813
  239.4 0.0 copy-start.13
  239.5 1.5 fusion.12
  241.0 0.2 copy-done.13
  241.3 1.3 fusion.18
  242.6 0.8 fusion.16
  243.4 2.5 %convert_element_type.26 = f32[512,2048]{1,0:T(8,128)} convert(bf16[512,2048]{1,0:T(8,128)(2,1)S(1)} %copy-done) | non-fusion elementwise | flops 1048576 | bytes 6291456 | tf_op jit(solution)/shard_map/convert_element_type | solution.py:835
  245.9 1.3 copy.57
  247.3 0.7 copy.58
  248.0 0.7 copy.59
  248.7 0.8 copy.60
  249.5 0.8 copy.61
  (35 shorter events, 0.1 us)
Async XLA Ops:
  8.3 226.7 %copy-start.16 = (f32[4,128]{1,0:T(4,128)S(1)}, f32[4,128]{1,0:T(4,128)}, u32[]{:S(2)}) copy-start(f32[4,128]{1,0:T(4,128)} %refs_3_.1) | copy-start | bytes 6148
  8.3 226.7 %copy-start.17 = (f32[4,128]{1,0:T(4,128)S(1)}, f32[4,128]{1,0:T(4,128)}, u32[]{:S(2)}) copy-start(f32[4,128]{1,0:T(4,128)} %param.39) | copy-start | bytes 6148
  8.4 226.8 %copy-start.18 = (f32[4,128]{1,0:T(4,128)S(1)}, f32[4,128]{1,0:T(4,128)}, u32[]{:S(2)}) copy-start(f32[4,128]{1,0:T(4,128)} %param.38) | copy-start | bytes 6148
  8.4 228.2 %copy-start.1 = (f32[128,1024]{1,0:T(8,128)S(1)}, f32[128,1024]{1,0:T(8,128)}, u32[]{:S(2)}) copy-start(f32[128,1024]{1,0:T(8,128)} %refs_6_.1) | copy-start | bytes 1572868
  235.0 4.4 %copy-start.2 = (f32[1024,128]{1,0:T(8,128)S(1)}, f32[1024,128]{1,0:T(8,128)}, u32[]{:S(2)}) copy-start(f32[1024,128]{1,0:T(8,128)} %refs_7_.1) | copy-start | bytes 1572868
  235.0 4.4 %copy-start.3 = (f32[1024,128]{1,0:T(8,128)S(1)}, f32[1024,128]{1,0:T(8,128)}, u32[]{:S(2)}) copy-start(f32[1024,128]{1,0:T(8,128)} %get-tuple-element.111) | copy-start | bytes 1572868
  235.1 4.4 %copy-start.8 = (f32[1024,128]{1,0:T(8,128)S(1)}, f32[1024,128]{1,0:T(8,128)}, u32[]{:S(2)}) copy-start(f32[1024,128]{1,0:T(8,128)} %param.37) | copy-start | bytes 1572868
  235.1 4.4 %copy-start.9 = (f32[1024,128]{1,0:T(8,128)S(1)}, f32[1024,128]{1,0:T(8,128)}, u32[]{:S(2)}) copy-start(f32[1024,128]{1,0:T(8,128)} %param.36) | copy-start | bytes 1572868
  239.4 1.6 copy-start.6
  239.4 1.6 copy-start.7
  239.4 1.6 copy-start.12
  239.4 1.8 copy-start.13
  241.0 1.6 copy-start.10
  241.0 1.6 copy-start.11
  241.0 1.6 copy-start.14
  241.0 1.6 copy-start.15
  241.0 2.4 copy-start
  243.4 2.5 %copy-start.5 = (bf16[512,2048]{1,0:T(8,128)(2,1)S(1)}, bf16[512,2048]{1,0:T(8,128)(2,1)}, u32[]{:S(2)}) copy-start(bf16[512,2048]{1,0:T(8,128)(2,1)} %get-tuple-element.94) | copy-start | bytes 6291460
  245.9 2.7 %copy-start.4 = (f32[128,1024]{1,0:T(8,128)S(1)}, f32[128,1024]{1,0:T(8,128)}, u32[]{:S(2)}) copy-start(f32[128,1024]{1,0:T(8,128)} %get-tuple-element.106) | copy-start | bytes 1572868

commit v2 on v1

v2 whole, which is shorter than its diff:
```python
import functools

import jax
import jax.numpy as jnp
from jax import lax
from jax.experimental import pallas as pl
from jax.experimental.pallas import tpu as pltpu
from jax.sharding import PartitionSpec as P

HD = 128
STEP = 5
ROWS = 512
D = 2048
NEG_FILL = -1e30
BETA_ONE = 0.5
BETA_TWO = 0.5
ADAM_EPS = 1e-08
NORM_EPS = 1e-05
DECAY_RATE = 0.1
RATE_QKV = 0.02
RATE_OUT = 0.15
RATE_UP = 0.02
RATE_DOWN = 0.01
RATE_NORMS = 0.3
SCALE = HD ** (-0.5)
GELU_K = 0.7978845608028654
GELU_C = 0.044715

BF = jnp.bfloat16
F32 = jnp.float32
MESH = pl.DeviceIdType.MESH
NT = (((1,), (1,)), ((), ()))
TN = (((0,), (0,)), ((), ()))
NN = (((1,), (0,)), ((), ()))

SHARD = ((128, 256), (128, 256), (128, 256), (256, 128), (128, 1024), (1024, 128))
Q_, K_, V_, O_, U_, D_ = range(6)
G_QKV = ((Q_, 0, 128, True), (K_, 0, 128, False), (V_, 0, 64, True), (V_, 64, 64, False))
G_OUT = ((O_, 0, 128, True), (O_, 128, 128, False))
G_UP = ((U_, 0, 64, True), (U_, 64, 64, False))
G_DOWN = ((D_, 0, 512, True), (D_, 512, 512, False))
GATHER = G_QKV + G_OUT + G_UP + G_DOWN
S_DOWN = ((D_, 0, 512, True), (D_, 512, 512, False))
S_UP = ((U_, 0, 64, True), (U_, 64, 64, False))
S_QKV = ((Q_, 0, 128, True), (K_, 0, 128, False), (V_, 0, 64, True), (V_, 64, 64, False))
S_OUT = ((O_, 0, 128, True), (O_, 128, 128, False))
SCATTER = S_DOWN + S_UP + S_QKV + S_OUT


def dot(a, b, dims=NN):
    return lax.dot_general(a, b, dims, preferred_element_type=F32)


def ds(start, size, mult=None):
    if not isinstance(start, int):
        start = pl.multiple_of(start, mult or size)
    return pl.ds(start, size)


N_SEND = 200
N_RECV = 140
N_LOCAL = 16


class Counter:
    def __init__(self):
        self.n = 0

    def take(self, k=1):
        base = self.n
        self.n += k
        return base


def kernel(*refs):
    it = iter(refs)
    take = lambda n: [next(it) for _ in range(n)]
    tok_h, cot_h, size_s, prefix_s, lens_s, nrm_in = take(6)
    wq_h, wo_h, wu_h, wd_h = take(4)
    bo_h, ig_h, gq_h, go_h, gu_h, gd_h, gn_o = take(7)
    wf_q, wf_o, wf_u, wf_d = take(4)
    own = take(6)
    gat = take(6)
    rcv1 = dict(zip(SCATTER, take(len(SCATTER))))
    rcv2 = dict(zip(SCATTER, take(len(SCATTER))))
    tok, back, bias, a1, qkv, mixed, probs, a2, hid, dup, slope, ps_a, ps_b, gdb = take(14)
    rc = take(3)
    rz = take(3)
    xown, r1, dr1, ybuf, dqkv, ds_s, nst, nbuf, gains, ngrad, nrec, oblk_b, oblk_i = take(13)
    ssem, rsem, lsem = take(3)
    rc = (rc[0], rc[1], rc[2], rc[0])
    rz = (rz[0], rz[1], rz[2], rz[0])
    dt, pb_s = tok, bias
    grad = {D_: gdb, **{k: gat[k] for k in (Q_, K_, V_, O_, U_)}}

    d_at = lax.axis_index("dp")
    t_at = lax.axis_index("tensor")
    x = d_at // 4
    yl = (d_at // 2) % 2
    c = d_at % 2
    z = t_at // 2
    yh = t_at % 2
    y = yh * 2 + yl
    other = 1 - c

    def dev(px, py, pz, pc):
        return {"dp": (px * 2 + py % 2) * 2 + pc, "tensor": pz * 2 + py // 2}

    nr, nl = Counter(), Counter()
    pending, free = [], list(range(N_SEND))[::-1]

    def rcopy(src, dst, to, si, ri):
        return pltpu.make_async_remote_copy(
            src_ref=src, dst_ref=dst, send_sem=ssem.at[si], recv_sem=rsem.at[ri],
            device_id=to, device_id_type=MESH)

    def send(src, dst, to, ri, tag=""):
        si = free.pop()
        cp = rcopy(src, dst, to, si, ri)
        cp.start()
        pending.append((tag, cp, None, si))

    def send_or_local(here, src, dst, to, ri, tag=""):
        si = free.pop()
        cp = rcopy(src, dst, to, si, ri)
        away = jnp.logical_not(here)

        @pl.when(here)
        def _():
            pltpu.make_async_copy(src, dst, rsem.at[ri]).start()

        @pl.when(away)
        def _():
            cp.start()

        pending.append((tag, cp, away, si))

    def send_if(cond, src, dst, to, ri, tag=""):
        si = free.pop()
        cp = rcopy(src, dst, to, si, ri)

        @pl.when(cond)
        def _():
            cp.start()

        pending.append((tag, cp, cond, si))

    def flush(tag=None):
        for item in pending[:]:
            kind, cp, cond, si = item
            if tag is None or kind == tag:
                pending.remove(item)
                free.append(si)
                if cond is None:
                    cp.wait_send()
                else:
                    pl.when(cond)(cp.wait_send)

    def got(dst, ri):
        rcopy(dst, dst, dev(x, y, z, other), 0, ri).wait_recv()

    def load(src, dst):
        cp = pltpu.make_async_copy(src, dst, lsem.at[nl.take()])
        cp.start()
        return cp

    home = c == yh
    my_row = c * 256 + z * 64
    ld_q = load(wq_h, wf_q)
    ld_o = load(wo_h, wf_o)
    ld_t = pltpu.make_async_copy(tok_h, tok, lsem.at[nl.take()])
    ld_c = pltpu.make_async_copy(cot_h, back, lsem.at[nl.take()])
    pl.when(home)(ld_t.start)
    ld_u = load(wu_h, wf_u)
    ld_d = load(wd_h, wf_d)
    pl.when(home)(ld_c.start)

    yp = yh * 2 + (1 - yl)
    peers = [dev(x, y, z, other)]
    for k in (1, 2, 3):
        for cc in (0, 1):
            peers.append(dev((x + k) % 4, y, z, cc))
            peers.append(dev(x, (y + k) % 4, z, cc))
            peers.append(dev(x, y, (z + k) % 4, cc))
            peers.append(dev((x + k) % 4, yp, z, cc))
    barrier = pltpu.get_barrier_semaphore()
    for peer in peers:
        pl.semaphore_signal(barrier, inc=1, device_id=peer, device_id_type=MESH)
    nst[0:4, :] = nrm_in[...].astype(BF).astype(F32)
    nst[4:8, :] = jnp.zeros((4, 128), F32)
    ld_q.wait()
    for j in range(3):
        own[j][...] = wf_q[j].astype(BF)
    ld_o.wait()
    own[O_][...] = wf_o[...].astype(BF)
    pl.when(home)(ld_t.wait)
    pl.semaphore_wait(barrier, len(peers))

    g1_r = {p: nr.take() for p in GATHER}
    g2_r = {p: nr.take(3) for p in GATHER}

    def gather_one(parts):
        for p in parts:
            k, r0, rn, x_first = p
            rows = pl.ds(r0, rn)
            for j in range(4):
                if x_first:
                    to = dev((x + j) % 4, y, z, yh)
                else:
                    to = dev(x, (y + j) % 4, z, yh)
                src, dst = own[k].at[rows], gat[k].at[x, yl, c, rows]
                if j == 0:
                    send_or_local(home, src, dst, to, g1_r[p], "gather")
                else:
                    send(src, dst, to, g1_r[p], "gather")

    r_at = (y + 4 - 2 * c) % 4

    def gather_two(parts):
        for p in parts:
            k, r0, rn, x_first = p
            rows = pl.ds(r0, rn)
            if x_first:
                part = gat[k].at[:, yl, :, rows]

                @pl.when(home)
                def _():
                    got(part, g1_r[p])

                for step in (1, 3):
                    send_if(home, part, part, dev(x, (y + step) % 4, z, c), g2_r[p], "gather")
            else:
                part = gat[k].at[x, :, :, rows]
                got(part, g1_r[p])
                send(part, part, dev((x + 1) % 4, y, z, c), g2_r[p], "gather")
                send(part, part, dev((x + 3) % 4, y, z, c), g2_r[p] + 1, "gather")

    def gather_three(parts):
        for p in parts:
            k, r0, rn, x_first = p
            rows = pl.ds(r0, rn)
            if x_first:
                src_l = 1 - r_at % 2
                got(gat[k].at[:, src_l, :, rows], g2_r[p])
                half = jnp.where((r_at == 0) | (r_at == 3), 1, 0)
                part = gat[k].at[pl.ds(2 * half, 2), src_l, :, rows]
                to = dev(x, (2 * c + 3 - r_at % 2) % 4, z, c)
                send(part, part, to, g2_r[p] + 1, "gather")
            else:
                xm, xp = (x + 3) % 4, (x + 1) % 4
                got(gat[k].at[xm, :, :, rows], g2_r[p])
                part = gat[k].at[xm, 0, :, rows]
                send(part, part, dev(xp, y, z, c), g2_r[p] + 2, "gather")
                got(gat[k].at[xp, :, :, rows], g2_r[p] + 1)
                part = gat[k].at[xp, 1, :, rows]
                send(part, part, dev(xm, y, z, c), g2_r[p] + 2, "gather")

    def gather_end(parts):
        for p in parts:
            k, r0, rn, x_first = p
            rows = pl.ds(r0, rn)
            if x_first:
                @pl.when(r_at >= 2)
                def _():
                    got(gat[k].at[:, r_at % 2, :, rows], g2_r[p] + 1)
            else:
                got(gat[k].at[(x + 2) % 4, :, :, rows], g2_r[p] + 2)

    gather_one(G_QKV)

    tok_r = nr.take(3)

    def share(i, buf):
        send_if(home, buf, buf, dev(x, y, z, other), tok_r + i, "group")

    def shared(i, buf):
        @pl.when(jnp.logical_not(home))
        def _():
            got(buf, tok_r + i)

    norm_r = nr.take()
    pltpu.make_async_copy(nst, nbuf.at[d_at], rsem.at[norm_r]).start()
    for dx in range(4):
        for dl in (0, 1):
            for dc in (0, 1):
                if dx or dl or dc:
                    to = dev((x + dx) % 4, yh * 2 + (yl + dl) % 2, z, (c + dc) % 2)
                    send(nst, nbuf.at[d_at], to, norm_r)
    share(0, tok)
    gather_one(G_OUT)

    ld_u.wait()

    @pl.loop(0, 8)
    def _(i):
        own[U_][ds(i * 16, 16), :] = wf_u[ds(i * 16, 16), :].astype(BF)

    @pl.when(home)
    def _():
        ends = []
        total = prefix_s[0]
        for i in range(16):
            total = total + jnp.where(i < size_s[0], lens_s[0, i], 0)
            ends.append(total)

        def segment(pos):
            seg = jnp.where(pos >= ends[0], 1, 0)
            for i in range(1, 16):
                seg = seg + jnp.where(pos >= ends[i], 1, 0)
            return jnp.where(pos < prefix_s[0], -1, seg)

        row_pos = lax.broadcasted_iota(jnp.int32, (8, ROWS), 1)
        row_seg = segment(row_pos)[0:1, :]
        row_pos = row_pos[0:1, :]

        @pl.loop(0, 8)
        def _(i):
            rows = ds(i * 64, 64)
            pos = lax.broadcasted_iota(jnp.int32, (64, 128), 0) + i * 64
            seg = jnp.concatenate([segment(pos)] * 4, axis=1)
            at = jnp.concatenate([pos] * 4, axis=1)
            linked = (seg == row_seg) | (row_seg < 0)
            live = (at < total) & (row_pos < total) & (row_pos <= at)
            allowed = (linked & live) | (row_pos == at)
            bias[rows, :] = jnp.where(allowed, 0.0, NEG_FILL).astype(BF)

        ld_c.wait()

        @pl.loop(0, 16)
        def _(i):
            rows = ds(i * 32, 32)
            pos = lax.broadcasted_iota(jnp.int32, (32, 128), 0) + i * 32
            keep = jnp.where(pos < total, 1.0, 0.0)
            keep = jnp.concatenate([keep] * 16, axis=1)
            back[rows, :] = (back[rows, :].astype(F32) * keep).astype(BF)

    share(1, bias)
    share(2, back)

    got(nbuf, norm_r)
    for i in range(16):
        gains[:, i * 128:(i + 1) * 128] = nbuf[i]

    gather_two(G_QKV)
    gather_one(G_UP)

    shared(0, tok)

    @pl.loop(0, ROWS // 32)
    def _(i):
        rows = ds(i * 32, 32)
        v = tok[rows, :].astype(F32)
        cen = v - jnp.mean(v, axis=-1, keepdims=True)
        var = jnp.mean(cen * cen, axis=-1, keepdims=True)
        a1[rows, :] = (cen * lax.rsqrt(var + NORM_EPS) * gains[0:1, :] + gains[1:2, :]).astype(BF)

    for i in range(4):
        xown[i * 16:(i + 1) * 16, :] = tok[ds(my_row + i * 16, 16), :]

    ld_d.wait()

    @pl.loop(0, 8)
    def _(i):
        own[D_][ds(i * 128, 128), :] = wf_d[ds(i * 128, 128), :].astype(BF)

    gather_three(G_QKV)
    gather_two(G_OUT)

    def project(j):
        v = dot(a1[...], gat[j][...].reshape(D, 256))
        if j == Q_:
            v = v * SCALE
        qkv[j] = v.astype(BF)

    gather_end(G_QKV)
    project(Q_)
    project(K_)
    project(V_)
    gather_three(G_OUT)
    gather_two(G_UP)
    gather_one(G_DOWN)
    shared(1, bias)

    for h in range(2):
        cols = slice(h * HD, (h + 1) * HD)

        @pl.loop(0, 4)
        def _(i):
            rows = ds(i * 128, 128)
            s = dot(qkv[0, rows, cols], qkv[1, :, cols], NT) + bias[rows, :].astype(F32)
            w = jnp.exp(s - jnp.max(s, axis=-1, keepdims=True))
            p = w / jnp.sum(w, axis=-1, keepdims=True)
            probs[h, rows, :] = p
            mixed[rows, cols] = dot(p.astype(BF), qkv[2, :, cols]).astype(BF)

    rc_r = [nr.take(4) for _ in range(4)]
    rz_r = [nr.take() for _ in range(4)]

    def sum_run(k, ps, compute):
        lo = other * 256

        def combine(j):
            cols = pl.ds(j * 512, 512)
            got(rc[k].at[j], rc_r[k] + j)
            for dz in (2, 1, 3, 0):
                pz = (z + dz) % 4
                rows = ds(c * 256 + pz * 64, 64)
                from_other = rc[k][j, ds(pz * 64, 64), :].astype(F32)
                ps[rows, cols] = (ps[rows, cols].astype(F32) + from_other).astype(BF)
                if dz:
                    send(ps.at[rows, cols], rz[k].at[dz - 1, :, cols], dev(x, y, pz, c),
                         rz_r[k], f"sum{k}")

        for j in range(4):
            cols = pl.ds(j * 512, 512)
            ps[:, cols] = compute(j).astype(BF)
            send(ps.at[ds(lo, 256), cols], rc[k].at[j], dev(x, y, z, other), rc_r[k] + j, f"sum{k}")
            if j:
                combine(j - 1)
        combine(3)

    def sum_wait(k):
        got(rz[k], rz_r[k])

    def sum_rows(k, ps, i):
        rows = ds(i * 16, 16)
        v = ps[ds(my_row + i * 16, 16), :].astype(F32)
        for j in range(3):
            v = v + rz[k][j, rows, :].astype(F32)
        return v

    ag_r = [nr.take(3) for _ in range(2)]
    ac_r = [nr.take() for _ in range(2)]

    def spread_start(k, buf):
        part = buf.at[ds(my_row, 64), :]
        for dz in (2, 1, 3):
            send(part, part, dev(x, y, (z + dz) % 4, c), ag_r[k] + dz - 1)
        send(part, part, dev(x, y, z, other), ac_r[k])

    def spread_pass(k, buf):
        for dz in (1, 3, 2):
            sz = (z + 4 - dz) % 4
            part = buf.at[ds(c * 256 + sz * 64, 64), :]
            got(part, ag_r[k] + dz - 1)
            send(part, part, dev(x, y, z, other), ac_r[k])

    def spread_end(k, buf):
        got(buf.at[ds(other * 256, 256), :], ac_r[k])

    def attn_out(j):
        w = jnp.concatenate([gat[O_][j, a, b] for a in range(2) for b in range(2)], axis=1)
        return dot(mixed[...], w)

    gather_end(G_OUT)
    flush("group")
    sum_run(0, ps_a, attn_out)
    gather_three(G_UP)
    gather_two(G_DOWN)
    sum_wait(0)

    @pl.loop(0, 4)
    def _(i):
        rows = ds(i * 16, 16)
        v = xown[rows, :].astype(F32) + sum_rows(0, ps_a, i)
        r1[rows, :] = v
        cen = v - jnp.mean(v, axis=-1, keepdims=True)
        var = jnp.mean(cen * cen, axis=-1, keepdims=True)
        n = cen * lax.rsqrt(var + NORM_EPS) * gains[2:3, :] + gains[3:4, :]
        a2[ds(my_row + i * 16, 16), :] = n.astype(BF)

    spread_start(0, a2)
    spread_pass(0, a2)
    gather_three(G_DOWN)

    gather_end(G_UP)
    spread_end(0, a2)

    @pl.loop(0, 4)
    def _(i):
        cols = ds(i * 256, 256)
        u = dot(a2[...], gat[U_][:, :, :, :, cols].reshape(D, 256))
        th = jnp.tanh(GELU_K * (u + GELU_C * u * u * u))
        hid[:, cols] = (0.5 * u * (1.0 + th)).astype(BF)
        slope[:, cols] = 0.5 * (1.0 + th) + 0.5 * u * (1.0 - th * th) * (GELU_K * (1.0 + 3.0 * GELU_C * u * u))

    shared(2, back)

    s1_r = {p: nr.take() for p in SCATTER}
    s2_r = {p: nr.take() for p in SCATTER}

    def scatter_one(parts):
        for p in parts:
            k, r0, rn, y_first = p
            rows = pl.ds(r0, rn)
            if y_first:
                for tl in range(2):
                    for tc in range(2):
                        here = home & (yl == tl) & (c == tc)
                        src, dst = grad[k].at[:, tl, tc, rows], rcv1[p].at[y]
                        send_or_local(here, src, dst, dev(x, 2 * c + tl, z, tc), s1_r[p])
            else:
                for dx in (2, 1, 3):
                    px = (x + dx) % 4
                    send(grad[k].at[px, :, :, rows], rcv1[p].at[dx - 1], dev(px, y, z, c), s1_r[p])

    def add_up(parts, out, shape):
        step = 16384 // shape[1]

        @pl.loop(0, shape[0] // step)
        def _(i):
            rows = ds(i * step, step)
            v = parts[0][rows, :].astype(F32)
            for q in parts[1:]:
                v = v + q[rows, :].astype(F32)
            out[rows, :] = v.astype(out.dtype)

    def scatter_two(parts):
        for p in parts:
            scatter_two_of(p)

    def scatter_two_of(p):
        k, r0, rn, y_first = p
        shape = (rn, SHARD[k][1])
        if y_first:
            got(rcv1[p], s1_r[p])
            for dx in (2, 1, 3, 0):
                px = (x + dx) % 4
                out = rcv1[p].at[0, px]
                add_up([rcv1[p].at[sy, px] for sy in range(4)], out, shape)
                if dx == 0:
                    pltpu.make_async_copy(out, rcv2[p].at[x], rsem.at[s2_r[p]]).start()
                else:
                    send(out, rcv2[p].at[x], dev(px, y, z, c), s2_r[p])
        else:
            got(rcv1[p], s1_r[p])
            for a in range(2):
                for b in range(2):
                    out = rcv1[p].at[0, a, b]
                    mine = grad[k].at[x, a, b, pl.ds(r0, rn)]
                    add_up([mine] + [rcv1[p].at[j, a, b] for j in range(3)], out, shape)
                    here = home & (yl == a) & (c == b)
                    send_or_local(here, out, rcv2[p].at[y], dev(x, 2 * c + a, z, b), s2_r[p])

    stage = {Q_: wf_q.at[0], K_: wf_q.at[1], V_: wf_q.at[2], O_: wf_o, U_: wf_u, D_: wf_d}

    def scatter_end(parts):
        for p in parts:
            k, r0, rn, _ = p
            got(rcv2[p], s2_r[p])
            add_up([rcv2[p].at[j] for j in range(4)], stage[k].at[pl.ds(r0, rn)], (rn, SHARD[k][1]))

    @pl.loop(0, 8)
    def _(i):
        v = dot(hid[...], back[:, ds(i * 256, 256)], TN).astype(BF)
        a, b = i // 2, i % 2
        gdb[a, b, 0] = v[:, :128]
        gdb[a, b, 1] = v[:, 128:]

    gather_end(G_DOWN)
    scatter_one(S_DOWN)

    @pl.loop(0, 4)
    def _(i):
        cols = ds(i * 256, 256)
        w = jnp.concatenate([gat[D_][a, b, e, cols, :] for a in range(4) for b in range(2) for e in range(2)], axis=1)
        dup[:, cols] = (dot(back[...], w, NT) * slope[:, cols]).astype(BF)

    def entry(j):
        return dot(dup[...], gat[U_][j].reshape(512, 1024), NT)

    def down(j):
        w = jnp.concatenate([gat[D_][j, a, b] for a in range(2) for b in range(2)], axis=1)
        return dot(hid[...], w)

    flush("sum0")
    sum_run(1, ps_a, entry)
    flush("gather")

    @pl.loop(0, 8)
    def _(i):
        a, b = i // 2, i % 2
        v = dot(a2[:, ds(i * 256, 256)], dup[...], TN).astype(BF)
        gat[U_][a, b, 0] = v[:128]
        gat[U_][a, b, 1] = v[128:]

    scatter_one(S_UP)

    def norm_back(v, dy, gain):
        cen = v - jnp.mean(v, axis=-1, keepdims=True)
        rs = lax.rsqrt(jnp.mean(cen * cen, axis=-1, keepdims=True) + NORM_EPS)
        xh = cen * rs
        e = dy * gain
        dv = rs * (e - jnp.mean(e, axis=-1, keepdims=True) - xh * jnp.mean(e * xh, axis=-1, keepdims=True))
        return dv, jnp.sum(dy * xh, axis=0, keepdims=True), jnp.sum(dy, axis=0, keepdims=True)

    ngrad[...] = jnp.zeros_like(ngrad)
    sum_wait(1)

    @pl.loop(0, 4)
    def _(i):
        rows = ds(i * 16, 16)
        mine = ds(my_row + i * 16, 16)
        dv, dg, db = norm_back(r1[rows, :], sum_rows(1, ps_a, i), gains[2:3, :])
        v = back[mine, :].astype(F32) + dv
        dr1[rows, :] = v
        dt[mine, :] = v.astype(BF)
        ngrad[2:3, :] += dg
        ngrad[3:4, :] += db

    spread_start(1, dt)

    o1_r = [nr.take(8) for _ in range(2)]

    def out_start(k, blk, out):
        part = out.at[ds(my_row, 64), :]
        for dz in (2, 1, 3):
            send(blk, part, dev(x, y, (z + dz) % 4, yh), o1_r[k] + z * 2 + c)
        send_or_local(home, blk, part, dev(x, y, z, yh), o1_r[k] + z * 2 + c)
        y2 = (y + 2) % 4
        send(blk, part, dev(x, y2, z, yh), o1_r[k] + z * 2 + c)

    def out_pass(k, out):
        away = jnp.logical_not(home)
        for sc in range(2):
            part = out.at[ds(sc * 256 + z * 64, 64), :]

            @pl.when(away)
            def _():
                got(part, o1_r[k] + z * 2 + sc)

            for dz in (2, 1, 3):
                send_if(away, part, part, dev(x, y, (z + dz) % 4, c), o1_r[k] + z * 2 + sc)

    def out_end(k, out):
        away = jnp.logical_not(home)
        for sc in range(2):
            for dz in range(4):
                sz = (z + dz) % 4

                def wait_it():
                    got(out.at[ds(sc * 256 + sz * 64, 64), :], o1_r[k] + sz * 2 + sc)

                if dz == 0:
                    pl.when(home)(wait_it)
                else:
                    wait_it()

    sum_run(2, ps_b, down)
    spread_pass(1, dt)
    spread_end(1, dt)

    @pl.loop(0, 2)
    def _(i):
        rows = ds(i * 256, 256)
        w = jnp.concatenate([gat[O_][a, b, e] for a in range(4) for b in range(2) for e in range(2)], axis=1)
        ybuf[rows, :] = dot(dt[rows, :], w, NT).astype(BF)

    for h in range(2):
        cols = slice(h * HD, (h + 1) * HD)

        @pl.loop(0, 4)
        def _(i):
            rows = ds(i * 128, 128)
            p = probs[h, rows, :]
            pb_s[rows, :] = p.astype(BF)
            dp = dot(ybuf[rows, cols], qkv[2, :, cols], NT)
            d_s = (p * (dp - jnp.sum(p * dp, axis=-1, keepdims=True))).astype(BF)
            ds_s[rows, :] = d_s
            dqkv[rows, cols] = dot(d_s, qkv[1, :, cols]).astype(BF)

        dqkv[:, 256 + h * HD:256 + (h + 1) * HD] = dot(ds_s[...], qkv[0, :, cols], TN).astype(BF)
        dqkv[:, 512 + h * HD:512 + (h + 1) * HD] = dot(pb_s[...], ybuf[:, cols], TN).astype(BF)

    def into_norm(j):
        ws = [gat[k][j].reshape(512, 256) for k in range(3)]
        v = dot(dqkv[:, 0:256], ws[0], NT) * SCALE
        v = v + dot(dqkv[:, 256:512], ws[1], NT)
        return v + dot(dqkv[:, 512:768], ws[2], NT)

    flush("sum1")
    sum_run(3, ps_a, into_norm)

    @pl.loop(0, 16)
    def _(i):
        a, b, e = i // 4, (i // 2) % 2, i % 2
        v = dot(a1[:, ds(i * 128, 128)], dqkv[...], TN)
        for k in range(3):
            w = v[:, k * 256:(k + 1) * 256]
            gat[k][a, b, e] = (w * SCALE if k == 0 else w).astype(BF)

    scatter_one(S_QKV)

    @pl.loop(0, 8)
    def _(i):
        v = dot(mixed[...], dt[:, ds(i * 256, 256)], TN).astype(BF)
        gat[O_][i // 2, i % 2, 0] = v[:, :128]
        gat[O_][i // 2, i % 2, 1] = v[:, 128:]

    scatter_one(S_OUT)
    sum_wait(2)

    @pl.loop(0, 4)
    def _(i):
        rows = ds(i * 16, 16)
        oblk_b[rows, :] = (r1[rows, :] + sum_rows(2, ps_b, i)).astype(BF)

    out_start(0, oblk_b, bo_h)
    scatter_two(S_DOWN)
    scatter_two(S_UP)

    sum_wait(3)

    @pl.loop(0, 4)
    def _(i):
        rows = ds(i * 16, 16)
        v = xown[rows, :].astype(F32)
        dv, dg, db = norm_back(v, sum_rows(3, ps_a, i), gains[0:1, :])
        oblk_i[rows, :] = (dr1[rows, :] + dv).astype(BF)
        ngrad[0:1, :] += dg
        ngrad[1:2, :] += db

    out_start(1, oblk_i, ig_h)

    n_r = [nr.take() for _ in range(3)]

    def norm_sum(stage, targets, base):
        for j, to in enumerate(targets):
            send(ngrad, nrec.at[base + j], to, n_r[stage], "norm")
        flush("norm")
        got(nrec.at[pl.ds(base, len(targets))], n_r[stage])
        v = ngrad[...]
        for j in range(len(targets)):
            v = v + nrec[base + j]
        ngrad[...] = v

    norm_sum(0, [dev(x, y, (z + dz) % 4, (c + dc) % 2) for dz in range(4) for dc in range(2) if dz or dc], 0)
    scatter_two(S_QKV)
    scatter_two(S_OUT)
    out_pass(0, bo_h)
    out_pass(1, ig_h)
    norm_sum(1, [dev((x + k) % 4, y, z, c) for k in (1, 2, 3)], 7)
    norm_sum(2, [dev(x, (y + k) % 4, z, c) for k in (1, 2, 3)], 10)
    gn_o[...] = ngrad[:, ds(d_at * 128, 128)]

    def put(src, dst):
        cp = pltpu.make_async_copy(src, dst, lsem.at[nl.take()])
        cp.start()
        return cp

    scatter_end(S_DOWN)
    puts = [put(wf_d, gd_h)]
    scatter_end(S_UP)
    puts.append(put(wf_u, gu_h))
    scatter_end(S_QKV)
    puts.append(put(wf_q, gq_h))
    scatter_end(S_OUT)
    puts.append(put(wf_o, go_h))
    out_end(0, bo_h)
    out_end(1, ig_h)
    for cp in puts:
        cp.wait()
    flush()
    assert nr.n <= N_RECV and nl.n <= N_LOCAL


def run_layer(tokens, cotangent, group_sizes, prefix_lens, solution_lens, norms, w_qkv, w_out, w_up, w_down):
    hbm = pl.BlockSpec(memory_space=pltpu.HBM)
    vmem = pl.BlockSpec(memory_space=pltpu.VMEM)
    smem = pl.BlockSpec(memory_space=pltpu.SMEM)
    buf = lambda s, t=BF: pltpu.VMEM(s, t)
    width = lambda p: (p[2], SHARD[p[0]][1])
    scratch = [buf((3, 128, 256), F32), buf((256, 128), F32), buf((128, 1024), F32), buf((1024, 128), F32)]
    scratch += [buf(s) for s in SHARD]
    scratch += [buf((4, 2, 2) + s) for s in SHARD]
    scratch += [buf(((4, 4) if p[3] else (3, 2, 2)) + width(p)) for p in SCATTER]
    scratch += [buf((4,) + width(p)) for p in SCATTER]
    scratch += [
        buf((ROWS, D)), buf((ROWS, D)), buf((ROWS, ROWS)), buf((ROWS, D)), buf((3, ROWS, 256)),
        buf((ROWS, 256)), buf((2, ROWS, ROWS), F32), buf((ROWS, D)), buf((ROWS, 1024)), buf((ROWS, 1024)),
        buf((ROWS, 1024), F32), buf((ROWS, D)), buf((ROWS, D)), buf((4, 2, 2, 1024, 128)),
    ]
    scratch += [buf((4, 256, 512))] * 3
    scratch += [buf((3, 64, D))] * 3
    scratch += [
        buf((64, D)), buf((64, D), F32), buf((64, D), F32), buf((ROWS, 256)), buf((ROWS, 768)),
        buf((ROWS, ROWS)), buf((8, 128), F32), buf((16, 8, 128), F32), buf((8, D), F32),
        buf((8, D), F32), buf((13, 8, D), F32), buf((64, D)), buf((64, D)),
    ]
    scratch += [pltpu.SemaphoreType.DMA((n,)) for n in (N_SEND, N_RECV, N_LOCAL)]
    out_shape = [
        jax.ShapeDtypeStruct((ROWS, D), BF), jax.ShapeDtypeStruct((ROWS, D), BF),
        jax.ShapeDtypeStruct((3, 128, 256), F32), jax.ShapeDtypeStruct((256, 128), F32),
        jax.ShapeDtypeStruct((128, 1024), F32), jax.ShapeDtypeStruct((1024, 128), F32),
        jax.ShapeDtypeStruct((8, 128), F32),
    ]
    return pl.pallas_call(
        kernel,
        out_shape=out_shape,
        in_specs=[hbm, hbm, smem, smem, smem, vmem, hbm, hbm, hbm, hbm],
        out_specs=[hbm] * 6 + [vmem],
        scratch_shapes=scratch,
        compiler_params=pltpu.CompilerParams(
            collective_id=0, has_side_effects=True, vmem_limit_bytes=63 * 2**20),
    )(tokens, cotangent, group_sizes, prefix_lens, solution_lens, norms, w_qkv, w_out, w_up, w_down)


def adamw(weight, grad_in, first_old, second_old, step_rate, weight_decay):
    first_new = BETA_ONE * first_old + (1.0 - BETA_ONE) * grad_in
    second_new = BETA_TWO * second_old + (1.0 - BETA_TWO) * grad_in * grad_in
    corr_one = 1.0 - BETA_ONE**STEP
    corr_two = 1.0 - BETA_TWO**STEP
    step_dir = first_new / corr_one / (jnp.sqrt(second_new / corr_two) + ADAM_EPS)
    weight_new = weight - step_rate * (step_dir + weight_decay * weight)
    return (grad_in, first_new, second_new, weight_new, weight_new.astype(jnp.bfloat16))


RATES = ((RATE_QKV, DECAY_RATE), (RATE_OUT, DECAY_RATE), (RATE_UP, DECAY_RATE), (RATE_DOWN, DECAY_RATE),
         (RATE_NORMS, 0.0))


def finish_kernel(bo, ig, *refs):
    ins, outs = refs[:20], refs[20:]
    outs[0][...] = bo[...]
    outs[1][...] = ig[...].astype(F32)
    for k, (rate, decay) in enumerate(RATES):
        w, g, m, v = (r[...] for r in ins[4 * k:4 * k + 4])
        if k == 4:
            g = g[0:4, :]
        for o, r in zip(outs[2 + 5 * k:7 + 5 * k], adamw(w, g, m, v, rate, decay)):
            o[...] = r


def finish(block_out, input_grad, sets):
    steps = 8
    whole = lambda s: pl.BlockSpec(s, lambda i: (0, 0))
    blocks = [
        pl.BlockSpec((3, 128 // steps, 256), lambda i: (0, i, 0)),
        pl.BlockSpec((256 // steps, 128), lambda i: (i, 0)),
        pl.BlockSpec((128 // steps, 1024), lambda i: (i, 0)),
        pl.BlockSpec((1024 // steps, 128), lambda i: (i, 0)),
        whole((4, 128)),
    ]
    rows = pl.BlockSpec((ROWS // steps, D), lambda i: (i, 0))
    in_specs, out_specs = [rows, rows], [rows, rows]
    out_shape = [jax.ShapeDtypeStruct((ROWS, D), BF), jax.ShapeDtypeStruct((ROWS, D), F32)]
    args = [block_out, input_grad]
    for spec, (w, g, m, v) in zip(blocks, sets):
        args += [w, g, m, v]
        in_specs += [spec, whole((8, 128)) if g.shape == (8, 128) else spec, spec, spec]
        out_specs += [spec] * 5
        out_shape += [jax.ShapeDtypeStruct(w.shape, F32)] * 4 + [jax.ShapeDtypeStruct(w.shape, BF)]
    return pl.pallas_call(
        finish_kernel, grid=(steps,), out_shape=out_shape, in_specs=in_specs, out_specs=out_specs,
        compiler_params=pltpu.CompilerParams(vmem_limit_bytes=63 * 2**20),
    )(*args)


def per_device(
    tokens, cotangent, group_sizes, prefix_lens, solution_lens,
    w_qkv, w_out, w_up, w_down, norms,
    first_qkv, second_qkv, first_out, second_out,
    first_up, second_up, first_down, second_down, first_norms, second_norms,
):
    block_out, input_grad, grad_qkv, grad_out, grad_up, grad_down, grad_norms = run_layer(
        tokens, cotangent, group_sizes, prefix_lens, solution_lens, norms, w_qkv, w_out, w_up, w_down)
    sets = (
        (w_qkv, grad_qkv, first_qkv, second_qkv),
        (w_out, grad_out, first_out, second_out),
        (w_up, grad_up, first_up, second_up),
        (w_down, grad_down, first_down, second_down),
        (norms, grad_norms, first_norms, second_norms),
    )
    return tuple(finish(block_out, input_grad, sets))


def solution(mesh):
    row, mat = P("dp", None), P("tensor", "dp")
    qkv, up, nrm = P(None, "dp", "tensor"), P("dp", "tensor"), P(None, "dp")
    return jax.shard_map(
        per_device,
        mesh=mesh,
        in_specs=(row, row, P("dp"), P("dp"), row, qkv, mat, up, mat, nrm,
                  qkv, qkv, mat, mat, up, up, mat, mat, nrm, nrm),
        out_specs=(row, row) + (qkv,) * 5 + (mat,) * 5 + (up,) * 5 + (mat,) * 5 + (nrm,) * 5,
        check_vma=False,
    )
```

time: 251 us -> 216 us (0.86)
  other arithmetic: 16.2 us -> 0 us
  Pallas kernels: 227 us -> 214 us
  local copies, waits for them, and re-layouts: 5.21 us -> 0 us
    pallas_call x1 -> x2, Pallas kernels: 227 us -> 214 us  [the longest x1 203 us: run_layer(): pl.pallas_call(kernel, out_shape=out_shape, in_specs=[hbm, hbm, smem, sme...]
    convert_element_type x7 -> x0, other arithmetic: 11.5 us -> none  [the longest x5 7.91 us: adamw(): weight_new.astype(jnp.bfloat16)]
    unnamed x43 -> x0, local copies, waits for them, and re-layouts: 4.61 us -> none
    select_n x2 -> x0, other arithmetic: 3.78 us -> none  [the longest x1 3.12 us: per_device(): jnp.where(valid_rows[:, None], cotangent, jnp.zeros_like(cotangent))]
where the time goes in v2:
time: 216 us
  Pallas kernels  214 us (99%)
    pallas_call x1, Pallas kernels, run_layer(): pl.pallas_call(kernel, out_shape=out_shape, in_specs=[hbm, hbm, smem, sme...  203 us
    pallas_call x1, Pallas kernels, finish(): pl.pallas_call(finish_kernel, grid=(steps,), out_shape=out_shape, in_spec...  11.2 us

profile of v2, /device:TPU:1, one launch (start us, length us, event | category | flops | bytes accessed | tf_op | source)
XLA Modules:
  0.0 216.1 jit_solution(5908609144527884699)
XLA Ops:
  2.0 202.7 %shard_map.403 = (bf16[512,2048]{1,0:T(8,128)(2,1)}, bf16[512,2048]{1,0:T(8,128)(2,1)}, f32[3,128,256]{2,1,0:T(8,128)}, f32[256,128]{1,0:T(8,128)}, f32[128,1024...) custom-call(bf16[512,2048]{1,0:T(8,128)(2,1)} %refs_0_.2, bf16[512,2048]{1,0:T(8,128)(2,1)} %refs_1_.1, ...), custom_call_target="tpu_custom_call" | custom-call | tf_op jit(solution)/shard_map/pallas_call | solution.py:797
  204.7 11.2 %shard_map.404 = (bf16[512,2048]{1,0:T(8,128)(2,1)}, f32[512,2048]{1,0:T(8,128)}, f32[3,128,256]{2,1,0:T(8,128)}, f32[3,128,256]{2,1,0:T(8,128)}, f32[3,128,256]...) custom-call(bf16[512,2048]{1,0:T(8,128)(2,1)} %get-tuple-element.34., ...), custom_call_target="tpu_custom_call" | custom-call | tf_op jit(solution)/shard_map/pallas_call | solution.py:853

commit v3 on v2

--- a/solution.py
+++ b/solution.py
@@ -35,11 +35,12 @@
 
 SHARD = ((128, 256), (128, 256), (128, 256), (256, 128), (128, 1024), (1024, 128))
 Q_, K_, V_, O_, U_, D_ = range(6)
-G_QKV = ((Q_, 0, 128, True), (K_, 0, 128, False), (V_, 0, 64, True), (V_, 64, 64, False))
+G_QK = ((Q_, 0, 64, True), (Q_, 64, 64, False), (K_, 0, 64, True), (K_, 64, 64, False))
+G_V = ((V_, 0, 64, True), (V_, 64, 64, False))
 G_OUT = ((O_, 0, 128, True), (O_, 128, 128, False))
 G_UP = ((U_, 0, 64, True), (U_, 64, 64, False))
 G_DOWN = ((D_, 0, 512, True), (D_, 512, 512, False))
-GATHER = G_QKV + G_OUT + G_UP + G_DOWN
+GATHER = G_QK + G_V + G_OUT + G_UP + G_DOWN
 S_DOWN = ((D_, 0, 512, True), (D_, 512, 512, False))
 S_UP = ((U_, 0, 64, True), (U_, 64, 64, False))
 S_QKV = ((Q_, 0, 128, True), (K_, 0, 128, False), (V_, 0, 64, True), (V_, 64, 64, False))
@@ -57,8 +58,9 @@
     return pl.ds(start, size)
 
 
+F_SUM, F_SPREAD, F_OUT = 0, 1, 1
 N_SEND = 200
-N_RECV = 140
+N_RECV = 180
 N_LOCAL = 16
 
 
@@ -86,10 +88,12 @@
     tok, back, bias, a1, qkv, mixed, probs, a2, hid, dup, slope, ps_a, ps_b, gdb = take(14)
     rc = take(3)
     rz = take(3)
+    relay = take(3)
     xown, r1, dr1, ybuf, dqkv, ds_s, nst, nbuf, gains, ngrad, nrec, oblk_b, oblk_i = take(13)
     ssem, rsem, lsem = take(3)
     rc = (rc[0], rc[1], rc[2], rc[0])
     rz = (rz[0], rz[1], rz[2], rz[0])
+    relay = (relay[0], relay[1], relay[2], relay[0])
     dt, pb_s = tok, bias
     grad = {D_: gdb, **{k: gat[k] for k in (Q_, K_, V_, O_, U_)}}
 
@@ -266,7 +270,8 @@
             else:
                 got(gat[k].at[(x + 2) % 4, :, :, rows], g2_r[p] + 2)
 
-    gather_one(G_QKV)
+    gather_one(G_QK)
+    gather_one(G_V)
 
     tok_r = nr.take(3)
 
@@ -341,7 +346,8 @@
     for i in range(16):
         gains[:, i * 128:(i + 1) * 128] = nbuf[i]
 
-    gather_two(G_QKV)
+    gather_two(G_QK)
+    gather_two(G_V)
     gather_one(G_UP)
 
     shared(0, tok)
@@ -363,7 +369,8 @@
     def _(i):
         own[D_][ds(i * 128, 128), :] = wf_d[ds(i * 128, 128), :].astype(BF)
 
-    gather_three(G_QKV)
+    gather_three(G_QK)
+    gather_three(G_V)
     gather_two(G_OUT)
 
     def project(j):
@@ -372,7 +379,8 @@
             v = v * SCALE
         qkv[j] = v.astype(BF)
 
-    gather_end(G_QKV)
+    gather_end(G_QK)
+    gather_end(G_V)
     project(Q_)
     project(K_)
     project(V_)
@@ -389,35 +397,64 @@
             rows = ds(i * 128, 128)
             s = dot(qkv[0, rows, cols], qkv[1, :, cols], NT) + bias[rows, :].astype(F32)
             w = jnp.exp(s - jnp.max(s, axis=-1, keepdims=True))
-            p = w / jnp.sum(w, axis=-1, keepdims=True)
-            probs[h, rows, :] = p
-            mixed[rows, cols] = dot(p.astype(BF), qkv[2, :, cols]).astype(BF)
+            probs[h, rows, :] = w / jnp.sum(w, axis=-1, keepdims=True)
+
+    for h in range(2):
+        cols = slice(h * HD, (h + 1) * HD)
+        mixed[:, cols] = dot(probs[h].astype(BF), qkv[2, :, cols]).astype(BF)
 
     rc_r = [nr.take(4) for _ in range(4)]
     rz_r = [nr.take() for _ in range(4)]
+    rl_r = [nr.take(4) for _ in range(4)]
+
+    def z_block(dz):
+        return c * 256 + (z + dz) % 4 * 64
+
+    def sum_combine(k, ps, j):
+        cols = pl.ds(j * 512, 512)
+        got(rc[k].at[j], rc_r[k] + j)
+        for dz in (2, 1, 3, 0):
+            rows = ds(z_block(dz), 64)
+            from_other = rc[k][j, ds((z + dz) % 4 * 64, 64), :].astype(F32)
+            ps[rows, cols] = (ps[rows, cols].astype(F32) + from_other).astype(BF)
+
+    def sum_relay(k, ps, j):
+        cols = pl.ds(j * 512, 512)
+        if not F_SUM:
+            for dz in (2, 1, 3):
+                send(ps.at[ds(z_block(dz), 64), cols], rz[k].at[dz - 1, :, cols], dev(x, y, (z + dz) % 4, c),
+                     rz_r[k], f"sum{k}")
+            return
+        for half, step in ((0, 1), (1, 3)):
+            send(ps.at[ds(z_block(2) + half * 32, 32), cols], relay[k].at[j, half],
+                 dev(x, y, (z + step) % 4, c), rl_r[k] + j, f"sum{k}")
+
+    def sum_pass(k, ps, j):
+        if not F_SUM:
+            return
+        cols = pl.ds(j * 512, 512)
+        got(relay[k].at[j], rl_r[k] + j)
+        for half, step in ((0, 1), (1, 3)):
+            rows = ds(z_block(step) + half * 32, 32)
+            ps[rows, cols] = (ps[rows, cols].astype(F32) + relay[k][j, half].astype(F32)).astype(BF)
+            send(ps.at[ds(z_block(step), 64), cols], rz[k].at[half, :, cols],
+                 dev(x, y, (z + step) % 4, c), rz_r[k], f"sum{k}")
+
+    def sum_part(k, ps, compute, j):
+        cols = pl.ds(j * 512, 512)
+        ps[:, cols] = compute(j).astype(BF)
+        half = ps.at[ds(other * 256, 256), cols]
+        send(half, rc[k].at[j], dev(x, y, z, other), rc_r[k] + j, f"sum{k}")
 
     def sum_run(k, ps, compute):
-        lo = other * 256
-
-        def combine(j):
-            cols = pl.ds(j * 512, 512)
-            got(rc[k].at[j], rc_r[k] + j)
-            for dz in (2, 1, 3, 0):
-                pz = (z + dz) % 4
-                rows = ds(c * 256 + pz * 64, 64)
-                from_other = rc[k][j, ds(pz * 64, 64), :].astype(F32)
-                ps[rows, cols] = (ps[rows, cols].astype(F32) + from_other).astype(BF)
-                if dz:
-                    send(ps.at[rows, cols], rz[k].at[dz - 1, :, cols], dev(x, y, pz, c),
-                         rz_r[k], f"sum{k}")
-
-        for j in range(4):
-            cols = pl.ds(j * 512, 512)
-            ps[:, cols] = compute(j).astype(BF)
-            send(ps.at[ds(lo, 256), cols], rc[k].at[j], dev(x, y, z, other), rc_r[k] + j, f"sum{k}")
-            if j:
-                combine(j - 1)
-        combine(3)
+        for j in range(7):
+            if j < 4:
+                sum_part(k, ps, compute, j)
+            if 1 <= j < 5:
+                sum_combine(k, ps, j - 1)
+                sum_relay(k, ps, j - 1)
+            if 2 <= j < 6:
+                sum_pass(k, ps, j - 2)
 
     def sum_wait(k):
         got(rz[k], rz_r[k])
@@ -425,7 +462,7 @@
     def sum_rows(k, ps, i):
         rows = ds(i * 16, 16)
         v = ps[ds(my_row + i * 16, 16), :].astype(F32)
-        for j in range(3):
+        for j in range(2 if F_SUM else 3):
             v = v + rz[k][j, rows, :].astype(F32)
         return v
 
@@ -434,16 +471,25 @@
 
     def spread_start(k, buf):
         part = buf.at[ds(my_row, 64), :]
-        for dz in (2, 1, 3):
-            send(part, part, dev(x, y, (z + dz) % 4, c), ag_r[k] + dz - 1)
+        for half, step in ((0, 1), (1, 3)):
+            send(part, part, dev(x, y, (z + step) % 4, c), ag_r[k] + half)
+        if not F_SPREAD:
+            send(part, part, dev(x, y, (z + 2) % 4, c), ag_r[k] + 2)
         send(part, part, dev(x, y, z, other), ac_r[k])
 
     def spread_pass(k, buf):
-        for dz in (1, 3, 2):
-            sz = (z + 4 - dz) % 4
-            part = buf.at[ds(c * 256 + sz * 64, 64), :]
-            got(part, ag_r[k] + dz - 1)
+        base = c * 256
+        for half, step in ((0, 1), (1, 3)):
+            at = base + (z + 4 - step) % 4 * 64
+            part = buf.at[ds(at, 64), :]
+            got(part, ag_r[k] + half)
+            piece = buf.at[ds(at + half * 32, 32), :]
+            if F_SPREAD:
+                send(piece, piece, dev(x, y, (z + step) % 4, c), ag_r[k] + 2)
             send(part, part, dev(x, y, z, other), ac_r[k])
+        part = buf.at[ds(base + (z + 2) % 4 * 64, 64), :]
+        got(part, ag_r[k] + 2)
+        send(part, part, dev(x, y, z, other), ac_r[k])
 
     def spread_end(k, buf):
         got(buf.at[ds(other * 256, 256), :], ac_r[k])
@@ -550,12 +596,11 @@
             got(rcv2[p], s2_r[p])
             add_up([rcv2[p].at[j] for j in range(4)], stage[k].at[pl.ds(r0, rn)], (rn, SHARD[k][1]))
 
-    @pl.loop(0, 8)
-    def _(i):
-        v = dot(hid[...], back[:, ds(i * 256, 256)], TN).astype(BF)
-        a, b = i // 2, i % 2
-        gdb[a, b, 0] = v[:, :128]
-        gdb[a, b, 1] = v[:, 128:]
+    @pl.loop(0, 4)
+    def _(i):
+        v = dot(hid[...], back[:, ds(i * 512, 512)], TN).astype(BF)
+        for n in range(4):
+            gdb[i, n // 2, n % 2] = v[:, n * 128:(n + 1) * 128]
 
     gather_end(G_DOWN)
     scatter_one(S_DOWN)
@@ -577,12 +622,11 @@
     sum_run(1, ps_a, entry)
     flush("gather")
 
-    @pl.loop(0, 8)
-    def _(i):
-        a, b = i // 2, i % 2
-        v = dot(a2[:, ds(i * 256, 256)], dup[...], TN).astype(BF)
-        gat[U_][a, b, 0] = v[:128]
-        gat[U_][a, b, 1] = v[128:]
+    @pl.loop(0, 4)
+    def _(i):
+        v = dot(a2[:, ds(i * 512, 512)], dup[...], TN).astype(BF)
+        for n in range(4):
+            gat[U_][i, n // 2, n % 2] = v[n * 128:(n + 1) * 128]
 
     scatter_one(S_UP)
 
@@ -612,42 +656,47 @@
 
     o1_r = [nr.take(8) for _ in range(2)]
 
+    def out_rows(out, sz, sc, first=0, rows=64):
+        return out.at[ds(sc * 256 + sz % 4 * 64 + first, rows), :]
+
     def out_start(k, blk, out):
         part = out.at[ds(my_row, 64), :]
-        for dz in (2, 1, 3):
-            send(blk, part, dev(x, y, (z + dz) % 4, yh), o1_r[k] + z * 2 + c)
-        send_or_local(home, blk, part, dev(x, y, z, yh), o1_r[k] + z * 2 + c)
-        y2 = (y + 2) % 4
-        send(blk, part, dev(x, y2, z, yh), o1_r[k] + z * 2 + c)
-
-    def out_pass(k, out):
-        away = jnp.logical_not(home)
+        send(blk, part, dev(x, (y + 2) % 4, z, yh), o1_r[k] + c)
+        for half, step in ((0, 1), (1, 3)):
+            send(blk, part, dev(x, y, (z + step) % 4, yh), o1_r[k] + 2 + half * 2 + c)
+        if not F_OUT:
+            send(blk, part, dev(x, y, (z + 2) % 4, yh), o1_r[k] + 6 + c)
+        send_or_local(home, blk, part, dev(x, y, z, yh), o1_r[k] + c)
+
+    def out_two(k, out):
         for sc in range(2):
-            part = out.at[ds(sc * 256 + z * 64, 64), :]
-
-            @pl.when(away)
-            def _():
-                got(part, o1_r[k] + z * 2 + sc)
-
-            for dz in (2, 1, 3):
-                send_if(away, part, part, dev(x, y, (z + dz) % 4, c), o1_r[k] + z * 2 + sc)
+            part = out_rows(out, z, sc)
+            got(part, o1_r[k] + sc)
+            for half, step in ((0, 1), (1, 3)):
+                send_if(jnp.logical_not(home), part, part, dev(x, y, (z + step) % 4, c),
+                        o1_r[k] + 2 + half * 2 + sc)
+            if not F_OUT:
+                send_if(jnp.logical_not(home), part, part, dev(x, y, (z + 2) % 4, c), o1_r[k] + 6 + sc)
+
+    def out_three(k, out):
+        for sc in range(2):
+            for half, step in ((0, 1), (1, 3)):
+                got(out_rows(out, z + 4 - step, sc), o1_r[k] + 2 + half * 2 + sc)
+                if not F_OUT:
+                    continue
+                piece = out_rows(out, z + 4 - step, sc, half * 32, 32)
+                send(piece, piece, dev(x, y, (z + step) % 4, c), o1_r[k] + 6 + sc)
 
     def out_end(k, out):
-        away = jnp.logical_not(home)
         for sc in range(2):
-            for dz in range(4):
-                sz = (z + dz) % 4
-
-                def wait_it():
-                    got(out.at[ds(sc * 256 + sz * 64, 64), :], o1_r[k] + sz * 2 + sc)
-
-                if dz == 0:
-                    pl.when(home)(wait_it)
-                else:
-                    wait_it()
-
-    sum_run(2, ps_b, down)
+            got(out_rows(out, z + 2, sc), o1_r[k] + 6 + sc)
+
+    for j in range(4):
+        sum_part(2, ps_b, down, j)
     spread_pass(1, dt)
+    for j in range(4):
+        sum_combine(2, ps_b, j)
+        sum_relay(2, ps_b, j)
     spread_end(1, dt)
 
     @pl.loop(0, 2)
@@ -679,35 +728,37 @@
         return v + dot(dqkv[:, 512:768], ws[2], NT)
 
     flush("sum1")
+    for j in range(4):
+        sum_pass(2, ps_b, j)
     sum_run(3, ps_a, into_norm)
-
-    @pl.loop(0, 16)
-    def _(i):
-        a, b, e = i // 4, (i // 2) % 2, i % 2
-        v = dot(a1[:, ds(i * 128, 128)], dqkv[...], TN)
+    sum_wait(2)
+
+    @pl.loop(0, 4)
+    def _(i):
+        rows = ds(i * 16, 16)
+        oblk_b[rows, :] = (r1[rows, :] + sum_rows(2, ps_b, i)).astype(BF)
+
+    out_start(0, oblk_b, bo_h)
+
+    @pl.loop(0, 4)
+    def _(i):
+        v = dot(mixed[...], dt[:, ds(i * 512, 512)], TN).astype(BF)
+        for n in range(4):
+            gat[O_][i, n // 2, n % 2] = v[:, n * 128:(n + 1) * 128]
+
+    scatter_one(S_OUT)
+
+    @pl.loop(0, 8)
+    def _(i):
+        v = dot(a1[:, ds(i * 256, 256)], dqkv[...], TN)
         for k in range(3):
             w = v[:, k * 256:(k + 1) * 256]
-            gat[k][a, b, e] = (w * SCALE if k == 0 else w).astype(BF)
+            w = (w * SCALE if k == 0 else w).astype(BF)
+            gat[k][i // 2, i % 2, 0] = w[:128]
+            gat[k][i // 2, i % 2, 1] = w[128:]
 
     scatter_one(S_QKV)
-
-    @pl.loop(0, 8)
-    def _(i):
-        v = dot(mixed[...], dt[:, ds(i * 256, 256)], TN).astype(BF)
-        gat[O_][i // 2, i % 2, 0] = v[:, :128]
-        gat[O_][i // 2, i % 2, 1] = v[:, 128:]
-
-    scatter_one(S_OUT)
-    sum_wait(2)
-
-    @pl.loop(0, 4)
-    def _(i):
-        rows = ds(i * 16, 16)
-        oblk_b[rows, :] = (r1[rows, :] + sum_rows(2, ps_b, i)).astype(BF)
-
-    out_start(0, oblk_b, bo_h)
-    scatter_two(S_DOWN)
-    scatter_two(S_UP)
+    out_two(0, bo_h)
 
     sum_wait(3)
 
@@ -720,27 +771,41 @@
         ngrad[0:1, :] += dg
         ngrad[1:2, :] += db
 
+    n_r = [nr.take() for _ in range(3)]
+    targets = (
+        [dev(x, y, (z + dz) % 4, (c + dc) % 2) for dz in range(4) for dc in range(2) if dz or dc],
+        [dev((x + k) % 4, y, z, c) for k in (1, 2, 3)],
+        [dev(x, (y + k) % 4, z, c) for k in (1, 2, 3)],
+    )
+    places = (0, 7, 10)
+
+    def norm_send(stage):
+        for j, to in enumerate(targets[stage]):
+            send(ngrad, nrec.at[places[stage] + j], to, n_r[stage], "norm")
+
+    def norm_add(stage):
+        flush("norm")
+        count = len(targets[stage])
+        got(nrec.at[pl.ds(places[stage], count)], n_r[stage])
+        v = ngrad[...]
+        for j in range(count):
+            v = v + nrec[places[stage] + j]
+        ngrad[...] = v
+
     out_start(1, oblk_i, ig_h)
-
-    n_r = [nr.take() for _ in range(3)]
-
-    def norm_sum(stage, targets, base):
-        for j, to in enumerate(targets):
-            send(ngrad, nrec.at[base + j], to, n_r[stage], "norm")
-        flush("norm")
-        got(nrec.at[pl.ds(base, len(targets))], n_r[stage])
-        v = ngrad[...]
-        for j in range(len(targets)):
-            v = v + nrec[base + j]
-        ngrad[...] = v
-
-    norm_sum(0, [dev(x, y, (z + dz) % 4, (c + dc) % 2) for dz in range(4) for dc in range(2) if dz or dc], 0)
+    norm_send(0)
+    out_three(0, bo_h)
+    scatter_two(S_DOWN)
+    out_two(1, ig_h)
+    norm_add(0)
+    norm_send(1)
+    scatter_two(S_UP)
+    out_three(1, ig_h)
+    norm_add(1)
+    norm_send(2)
+    scatter_two(S_OUT)
     scatter_two(S_QKV)
-    scatter_two(S_OUT)
-    out_pass(0, bo_h)
-    out_pass(1, ig_h)
-    norm_sum(1, [dev((x + k) % 4, y, z, c) for k in (1, 2, 3)], 7)
-    norm_sum(2, [dev(x, (y + k) % 4, z, c) for k in (1, 2, 3)], 10)
+    norm_add(2)
     gn_o[...] = ngrad[:, ds(d_at * 128, 128)]
 
     def put(src, dst):
@@ -781,7 +846,8 @@
         buf((ROWS, 1024), F32), buf((ROWS, D)), buf((ROWS, D)), buf((4, 2, 2, 1024, 128)),
     ]
     scratch += [buf((4, 256, 512))] * 3
-    scratch += [buf((3, 64, D))] * 3
+    scratch += [buf((2 if F_SUM else 3, 64, D))] * 3
+    scratch += [buf((4, 2, 32, 512))] * 3
     scratch += [
         buf((64, D)), buf((64, D), F32), buf((64, D), F32), buf((ROWS, 256)), buf((ROWS, 768)),
         buf((ROWS, ROWS)), buf((8, 128), F32), buf((16, 8, 128), F32), buf((8, D), F32),
@@ -832,7 +898,7 @@
 
 
 def finish(block_out, input_grad, sets):
-    steps = 8
+    steps = 2
     whole = lambda s: pl.BlockSpec(s, lambda i: (0, 0))
     blocks = [
         pl.BlockSpec((3, 128 // steps, 256), lambda i: (0, i, 0)),

time: 216 us -> 206 us (0.954)
  Pallas kernels: 214 us -> 204 us
    pallas_call x1, Pallas kernels: 203 us -> 196 us  [run_layer(): pl.pallas_call(kernel, out_shape=out_shape, in_specs=[hbm, hbm, smem, sme...]
    pallas_call x1, Pallas kernels: 11.2 us -> 8.35 us  [finish(): pl.pallas_call(finish_kernel, grid=(steps,), out_shape=out_shape, in_spec...]
where the time goes in v3:
time: 206 us
  Pallas kernels  204 us (99%)
  between operations  2.13 us (1%)
    pallas_call x1, Pallas kernels, run_layer(): pl.pallas_call(kernel, out_shape=out_shape, in_specs=[hbm, hbm, smem, sme...  196 us
    pallas_call x1, Pallas kernels, finish(): pl.pallas_call(finish_kernel, grid=(steps,), out_shape=out_shape, in_spec...  8.35 us

profile of v3, /device:TPU:1, one launch (start us, length us, event | category | flops | bytes accessed | tf_op | source)
XLA Modules:
  0.0 206.1 jit_solution(14558432052608990901)
XLA Ops:
  2.0 195.6 %shard_map.403 = (bf16[512,2048]{1,0:T(8,128)(2,1)}, bf16[512,2048]{1,0:T(8,128)(2,1)}, f32[3,128,256]{2,1,0:T(8,128)}, f32[256,128]{1,0:T(8,128)}, f32[128,1024...) custom-call(bf16[512,2048]{1,0:T(8,128)(2,1)} %refs_0_.2, bf16[512,2048]{1,0:T(8,128)(2,1)} %refs_1_.1, ...), custom_call_target="tpu_custom_call" | custom-call | tf_op jit(solution)/shard_map/pallas_call | solution.py:863
  197.6 8.3 %shard_map.404 = (bf16[512,2048]{1,0:T(8,128)(2,1)}, f32[512,2048]{1,0:T(8,128)}, f32[3,128,256]{2,1,0:T(8,128)}, f32[3,128,256]{2,1,0:T(8,128)}, f32[3,128,256]...) custom-call(bf16[512,2048]{1,0:T(8,128)(2,1)} %get-tuple-element.34., ...), custom_call_target="tpu_custom_call" | custom-call | tf_op jit(solution)/shard_map/pallas_call | solution.py:919

commit v4 on v3

--- a/solution.py
+++ b/solution.py
@@ -348,7 +348,6 @@
 
     gather_two(G_QK)
     gather_two(G_V)
-    gather_one(G_UP)
 
     shared(0, tok)
 
@@ -372,6 +371,7 @@
     gather_three(G_QK)
     gather_three(G_V)
     gather_two(G_OUT)
+    gather_one(G_UP)
 
     def project(j):
         v = dot(a1[...], gat[j][...].reshape(D, 256))
@@ -757,7 +757,7 @@
             gat[k][i // 2, i % 2, 0] = w[:128]
             gat[k][i // 2, i % 2, 1] = w[128:]
 
-    scatter_one(S_QKV)
+    scatter_one([p for p in S_QKV if not p[3]])
     out_two(0, bo_h)
 
     sum_wait(3)
@@ -793,17 +793,18 @@
         ngrad[...] = v
 
     out_start(1, oblk_i, ig_h)
+    scatter_one([p for p in S_QKV if p[3]])
     norm_send(0)
     out_three(0, bo_h)
     scatter_two(S_DOWN)
-    out_two(1, ig_h)
     norm_add(0)
     norm_send(1)
+    out_two(1, ig_h)
     scatter_two(S_UP)
-    out_three(1, ig_h)
+    scatter_two(S_OUT)
     norm_add(1)
     norm_send(2)
-    scatter_two(S_OUT)
+    out_three(1, ig_h)
     scatter_two(S_QKV)
     norm_add(2)
     gn_o[...] = ngrad[:, ds(d_at * 128, 128)]

time: 206 us -> 204 us (level)
  Pallas kernels: 204 us -> 201 us
    pallas_call x1, Pallas kernels: 196 us -> 193 us  [run_layer(): pl.pallas_call(kernel, out_shape=out_shape, in_specs=[hbm, hbm, smem, sme...]
where the time goes in v4:
time: 204 us
  Pallas kernels  201 us (99%)
  between operations  2.13 us (1%)
    pallas_call x1, Pallas kernels, run_layer(): pl.pallas_call(kernel, out_shape=out_shape, in_specs=[hbm, hbm, smem, sme...  193 us
    pallas_call x1, Pallas kernels, finish(): pl.pallas_call(finish_kernel, grid=(steps,), out_shape=out_shape, in_spec...  8.35 us

profile of v4, /device:TPU:1, one launch (start us, length us, event | category | flops | bytes accessed | tf_op | source)
XLA Modules:
  0.0 203.6 jit_solution(8488953336806216810)
XLA Ops:
  2.0 193.1 %shard_map.403 = (bf16[512,2048]{1,0:T(8,128)(2,1)}, bf16[512,2048]{1,0:T(8,128)(2,1)}, f32[3,128,256]{2,1,0:T(8,128)}, f32[256,128]{1,0:T(8,128)}, f32[128,1024...) custom-call(bf16[512,2048]{1,0:T(8,128)(2,1)} %refs_0_.2, bf16[512,2048]{1,0:T(8,128)(2,1)} %refs_1_.1, ...), custom_call_target="tpu_custom_call" | custom-call | tf_op jit(solution)/shard_map/pallas_call | solution.py:864
  195.1 8.3 %shard_map.404 = (bf16[512,2048]{1,0:T(8,128)(2,1)}, f32[512,2048]{1,0:T(8,128)}, f32[3,128,256]{2,1,0:T(8,128)}, f32[3,128,256]{2,1,0:T(8,128)}, f32[3,128,256]...) custom-call(bf16[512,2048]{1,0:T(8,128)(2,1)} %get-tuple-element.34., ...), custom_call_target="tpu_custom_call" | custom-call | tf_op jit(solution)/shard_map/pallas_call | solution.py:920
